TPU v7x, 512 devices: a whole 4x8x8 slice. The times are simulated.
512 devices in a mesh: section: 16 (over z, x_hi), tensor: 32 (over x_lo, y, core).
Axes of the slice: x: 4 (x_hi: 2, x_lo: 2; x = x_hi * 2 + x_lo), y: 8, z: 8, core: 2. Of those that a mesh axis runs over, the one named last changes fastest.
Arguments:
- hidden: bfloat16 [4, 52, 4608], P(None, None, 'tensor'), may hold values from -6 to 6
- weight: bfloat16 [139264, 4608], P(('section', 'tensor')), may hold values from -1 to 1
- targets: int32 [4, 52], replicated, may hold values from 0 to 139263
- plan: int32 [4], replicated, may hold values from 0 to 3, each once
- row_grad: float32 [4, 52], replicated, may hold values from -4 to 4
Outputs:
- logprob: float32 [4, 52], replicated
- hidden_grad: bfloat16 [4, 52, 4608], P(None, None, 'tensor')
- weight_grad: bfloat16 [139264, 4608], P(('section', 'tensor'))
- target_scale: float32 [4, 52], replicated
All inputs are finite; a program needn't handle non-finite values.
Results may differ from a plain program's by a relative error of at most 0.015.
Values may be sent and summed in bfloat16 or wider, within the bound.
A program may use at most 64 MiB of HBM per device.

v0:
```python
import jax
import jax.numpy as jnp
from jax import lax
from jax.sharding import PartitionSpec as P

softcap_value = 30.0


def per_device(hidden, weight, targets, plan, row_grad):
    micro_count = hidden.shape[0]
    row_span = hidden.shape[1]
    row_count = micro_count * row_span
    vocab_dev = weight.shape[0]
    select = plan[:, None] == jnp.arange(micro_count, dtype=jnp.int32)[None, :]
    order_targets = jnp.sum(jnp.where(select[:, :, None], targets[None], 0), axis=1).reshape(-1)
    order_grad = jnp.sum(
        jnp.where(select[:, :, None], row_grad[None], jnp.float32(0.0)), axis=1
    ).reshape(-1)
    contract_features = (((1,), (1,)), ((), ()))
    contract_rows = (((0,), (0,)), ((), ()))
    gathered = lax.all_gather(hidden, "tensor", axis=2, tiled=True)
    flat_rows = gathered.reshape(row_count, gathered.shape[2])
    raw_logits = lax.dot_general(
        flat_rows, weight, contract_features, preferred_element_type=jnp.float32
    )
    capped = softcap_value * jnp.tanh(raw_logits / softcap_value)
    vocab_ids = lax.axis_index(("section", "tensor")) * vocab_dev + jnp.arange(
        vocab_dev, dtype=jnp.int32
    )
    target_hit = vocab_ids[None, :] == order_targets[:, None]
    exponent = jnp.exp(capped)
    local_total = jnp.sum(exponent, axis=1)
    local_target = jnp.sum(jnp.where(target_hit, capped, jnp.float32(0.0)), axis=1)
    total, target_logit = lax.psum((local_total, local_target), ("section", "tensor"))
    slot_logprob = (target_logit - jnp.log(total)).reshape(micro_count, row_span)
    logprob = jnp.sum(
        jnp.where(select[:, :, None], slot_logprob[:, None, :], jnp.float32(0.0)), axis=0
    )
    slot_scale = (order_grad * (1.0 - jnp.square(target_logit / softcap_value))).reshape(
        micro_count, row_span
    )
    target_scale = jnp.sum(
        jnp.where(select[:, :, None], slot_scale[:, None, :], jnp.float32(0.0)), axis=0
    )
    probability = exponent / total[:, None]
    curve = 1.0 - jnp.square(capped / softcap_value)
    scaled = order_grad[:, None] * (target_hit.astype(jnp.float32) - probability)
    logit_grad = (scaled * curve).astype(jnp.bfloat16)
    negative = -(order_grad[:, None] * probability)
    soft_grad = (negative * curve).astype(jnp.bfloat16)
    grad_terms = jnp.dot(logit_grad, weight, preferred_element_type=jnp.float32).reshape(
        micro_count, row_span, weight.shape[1]
    )
    section_total = lax.psum(grad_terms, "section")
    summed = lax.psum_scatter(section_total, "tensor", scatter_dimension=2, tiled=True)
    hidden_grad = summed.astype(jnp.bfloat16)
    weight_grad = lax.dot_general(
        soft_grad, flat_rows, contract_rows, preferred_element_type=jnp.float32
    ).astype(jnp.bfloat16)
    return (logprob, hidden_grad, weight_grad, target_scale)


def solution(mesh):
    placed = (P(None, None, "tensor"), P(("section", "tensor"), None), P(), P(), P())
    return jax.shard_map(
        per_device,
        mesh=mesh,
        in_specs=placed,
        out_specs=(P(), P(None, None, "tensor"), P(("section", "tensor"), None), P()),
        check_vma=False,
    )
```

profile of v0, /device:TPU:2, one launch (start us, length us, event | category | flops | bytes accessed | tf_op | source)
XLA Modules:
  0.0 428.5 jit_solution(12417458577136251588)
XLA Ops:
  7.2 1.9 copy.15
  9.2 0.0 reduce-scatter.4.cloned.1.call-start
  9.2 0.7 iota_compare_fusion
  9.9 0.8 select_reduce_fusion.1
  10.7 0.1 mul.37
  10.8 0.8 select_reduce_fusion.3
  11.6 0.1 eq.36
  11.7 73.4 %all-gather.2.cloned.1.call-done = bf16[4,52,4608]{1,0,2:T(4,128)(2,1)} async-done(((bf16[4,52,144]{1,0,2:T(4,128)(2,1)}), bf16[4,52,4608]{1,0,2:T(4,128)(2,1)}) %all-gather.2.cloned.1.call-update) | async-done | bytes 1916944 | tf_op jit(solution)/shard_map/all_gather | solution.py:21
  85.1 7.5 %reshape.49 = bf16[208,4608]{0,1:T(8,128)(2,1)} reshape(bf16[4,52,4608]{1,0,2:T(4,128)(2,1)} %all-gather.2.cloned.1.call-done) | data formatting | bytes 3833856 | tf_op jit(solution)/shard_map/reshape | solution.py:22
  92.6 2.5 exponential_reduce_fusion
  95.1 98.9 %all-reduce = (f32[208]{0:T(256)S(1)}, f32[208]{0:T(256)S(1)}) all-reduce(f32[208]{0:T(256)S(1)} %get-tuple-element.17, f32[208]{0:T(256)S(1)} %get-tuple-element.16), channel_id=1, replica_groups=mesh['section'=16,'tensor'=32] {'section','tensor'}, use_global_device_ids=true, to_apply=%region_2.3 | all-reduce | flops 416 | bytes 3328 | tf_op jit(solution)/shard_map/psum | solution.py:34
  193.9 3.1 fusion.6
  197.1 3.8 reshape.48
  200.8 9.4 %copy.19 = f32[4,52,4608]{1,0,2:T(4,128)} copy(f32[4,52,4608]{2,1,0:T(8,128)} %reshape.48) | data formatting | bytes 7667712
  210.2 9.3 %reshape.50 = f32[4608,208]{1,0:T(8,128)} reshape(f32[4608,4,52]{2,1,0:T(4,128)} %bitcast.8) | data formatting | bytes 7667712
  219.5 0.1 broadcast_in_dim.85
  219.6 0.1 broadcast_in_dim.89
  219.7 0.7 select_reduce_fusion
  220.3 4.0 convolution_convert_fusion
  224.3 115.4 %reduce-scatter.4.cloned.1.call-done = f32[144,208]{1,0:T(8,128)} async-done(((f32[4608,208]{1,0:T(8,128)}), f32[144,208]{1,0:T(8,128)}) %reduce-scatter.4.cloned.1.call-update) | async-done | bytes 119824
  339.7 1.1 reshape.51
  340.8 0.2 copy.20
  341.0 79.9 %psum.24 = bf16[4,52,144]{2,1,0:T(8,128)(2,1)S(1)} all-reduce(f32[4,52,144]{2,1,0:T(8,128)S(1)} %copy.20), channel_id=1, replica_groups=mesh['section'=16,'tensor'=32] {'section'}, use_global_device_ids=true, to_apply=%region_7.8 | all-reduce | flops 29952 | bytes 179712 | tf_op jit(solution)/shard_map/psum | solution.py:54
  420.9 0.7 copy.17
  (7 shorter events, 0.1 us)
Async XLA Ops:
  7.2 85.4 %copy-start = (bf16[272,4608]{1,0:T(8,128)(2,1)S(1)}, bf16[272,4608]{1,0:T(8,128)(2,1)}, u32[]{:S(2)}) copy-start(bf16[272,4608]{1,0:T(8,128)(2,1)} %param.6) | copy-start | bytes 7520260
  7.2 77.9 %all-gather.2.cloned.1.call-start = ((), (), s32[]{:S(2)}) async-start(), calls=%async_computation.1 | async-start | bytes 4866048 | tf_op jit(solution)/shard_map/all_gather | solution.py:21
  9.2 330.6 %reduce-scatter.4.cloned.1.call-start = ((), (), s32[]{:S(2)}) async-start(), calls=%async_computation.2 | async-start | bytes 4866048
Sparse Core Ops, SparseCore 0:
  10.7 74.3 all-gather.1
  219.6 120.0 reduce-scatter.3
where the time goes:
time: 429 us; the launch traced here: 428 us
  waiting for transfers between devices  189 us (44%)
  blocking collectives  179 us (42%)
  local copies, waits for them, and re-layouts  34.1 us (8%)
  between operations  14.1 us (3%)
  matrix products  9.63 us (2%)
    unnamed x3, waiting for transfers between devices  115 us
    psum x1, blocking collectives, per_device(): lax.psum((local_total, local_target), ('section', 'tensor'))  98.9 us
    psum x1, blocking collectives, per_device(): section_total = lax.psum(grad_terms, 'section')  79.9 us
    all_gather x1, waiting for transfers between devices, per_device(): gathered = lax.all_gather(hidden, 'tensor', axis=2, tiled=True)  73.4 us
    unnamed x8, local copies, waits for them, and re-layouts  22.5 us
  transfers between devices with their start and end apart: 2, of which 2 were waited for; matrix products, arithmetic and copies ran while one was open for 2% of the time, Pallas kernels for 0%

commit v1 on v0

v1 whole, which is shorter than its diff:
```python
import functools

import jax
import jax.numpy as jnp
from jax import lax
from jax.experimental import pallas as pl
from jax.experimental.pallas import tpu as pltpu
from jax.sharding import PartitionSpec as P

MESH = pl.DeviceIdType.MESH
CAP = 30.0
F32 = jnp.float32
BF16 = jnp.bfloat16
MICRO = 4
ROWS = 52
SLOT = 64
V = 272
D = 4608
SH = 144
NEAR = (1, 7, 2, 6, 3, 5, 4)
FAR = (4, 3, 5, 2, 6, 1, 7)


def coords():
    s = lax.axis_index("section")
    t = lax.axis_index("tensor")
    x_hi, z = lax.rem(s, 2), lax.div(s, 2)
    q, y, c = lax.div(t, 16), lax.rem(lax.div(t, 2), 8), lax.rem(t, 2)
    return x_hi * 2 + q, y, z, c


def dev(x, y, z, c):
    x, y, z, c = lax.rem(x + 4, 4), lax.rem(y + 8, 8), lax.rem(z + 8, 8), lax.rem(c + 2, 2)
    return (z * 2 + lax.div(x, 2), lax.rem(x, 2) * 16 + y * 2 + c)


def rcopy(src, dst, ss, rs, to):
    return pltpu.make_async_remote_copy(
        src_ref=src, dst_ref=dst, send_sem=ss, recv_sem=rs, device_id=to, device_id_type=MESH
    )


def slot_lanes(ref, plan_ref, fill, dtype):
    parts = []
    for k in range(MICRO):
        row = jnp.zeros((1, SLOT), dtype)
        for j in range(MICRO):
            row = jnp.where(plan_ref[k] == j, ref[pl.ds(j, 1), :], row)
        parts.append(row)
    wide = jnp.concatenate(parts, axis=1)
    lane = lax.broadcasted_iota(jnp.int32, (1, 4 * SLOT), 1)
    return jnp.where(lax.rem(lane, SLOT) < ROWS, wide, jnp.full_like(wide, fill))


def comm_kernel(
    hidden_ref, weight_ref, targets_ref, plan_ref, grad_ref,
    ht_ref, soft_ref, hg_ref, stat_ref,
    pad, h, w, wt, own, ctx, crx, xtx, xrx, ztx, zrx, ytx, yrx, rtx, rrx, atx, arx, tot_tx, tot_rx,
    w_sem, o_sem,
    gy_s, gy_r, gz_s, gz_r, gx_s, gx_r, gc_s, gc_r,
    t_s, t_r, c_s, c_r, x_s, x_r, z_s, z_r, y_s, y_r, r_s, r_r, a_s, a_r, b_s, b_r,
):
    x, y, z, c = coords()
    q, x_hi, p, zq = lax.rem(x, 2), lax.div(x, 2), lax.rem(z, 2), lax.div(z, 2)
    other = 1 - q
    me = q * 16 + y * 2 + c
    partner = dev(x, y, z, 1 - c)

    barrier = pltpu.get_barrier_semaphore()
    peers = [dev(x, y + d, z, c) for d in range(1, 8)]
    peers += [dev(x + a, y, z, c + b) for a in range(4) for b in range(2) if a or b]
    peers += [dev(x + 2 * a, y, z + d, c) for d in range(1, 8) for a in range(2)]
    for peer in peers:
        pl.semaphore_signal(barrier, inc=1, device_id=peer, device_id_type=MESH)
    w_copy = pltpu.make_async_copy(weight_ref, w, w_sem)
    w_copy.start()

    pad[...] = jnp.zeros_like(pad)
    for k in range(MICRO):
        pad[k * SLOT : k * SLOT + ROWS, 0:SH] = hidden_ref[k].astype(F32)
    mine = jnp.transpose(pad[...], (1, 0))[0:SH]
    h[0, me] = mine[:, 0:128].astype(BF16)
    h[1, me] = mine[:, 128:256].astype(BF16)
    slot_target = slot_lanes(targets_ref, plan_ref, -1, jnp.int32)
    slot_grad = slot_lanes(grad_ref, plan_ref, 0.0, F32)
    pl.semaphore_wait(barrier, len(peers))

    def shard(x_lo, yy):
        return x_lo * 16 + yy * 2 + c

    def y_copy(yy, to_y):
        t = shard(q, yy)
        return rcopy(h.at[p, t], h.at[p, t], gy_s.at[to_y], gy_r.at[yy], dev(x, to_y, z, c))

    def z_copy(yy, half):
        t = shard(q, yy)
        return rcopy(h.at[half, t], h.at[half, t], gz_s.at[yy], gz_r.at[yy], dev(x, y, z + 1 - 2 * lax.rem(yy, 2), c))

    def x_copy(x_lo, yy, half):
        t = shard(x_lo, yy)
        return rcopy(h.at[half, t], h.at[half, t], gx_s.at[half, yy], gx_r.at[half, yy], dev(x + 1 - 2 * half, y, z, c))

    def c_copy(x_lo, yy, cc, half):
        t = x_lo * 16 + yy * 2 + cc
        i = x_lo * 8 + yy
        return rcopy(h.at[half, t], h.at[half, t], gc_s.at[half, i], gc_r.at[half, i], partner)

    def at_y(d):
        return lax.rem(y + d, 8)

    for d in FAR:
        y_copy(y, at_y(d)).start()
    for half in range(2):
        x_copy(q, y, half).start()
        c_copy(q, y, c, half).start()
    w_copy.wait()
    for j in range(D // 128):
        wt[j * 128 : (j + 1) * 128, :] = jnp.transpose(w[:, j * 128 : (j + 1) * 128], (1, 0))
    for d in NEAR:
        yy = at_y(d)
        y_copy(yy, y).wait_recv()
        z_copy(yy, p).start()
        x_copy(q, yy, p).start()
        c_copy(q, yy, c, p).start()
    for d in NEAR:
        yy = at_y(d)
        z_copy(yy, 1 - p).wait_recv()
        x_copy(q, yy, 1 - p).start()
        c_copy(q, yy, c, 1 - p).start()
    for d in (0,) + NEAR:
        yy = at_y(d)
        for half in range(2):
            x_copy(other, yy, half).wait_recv()
            c_copy(other, yy, c, half).start()

    def block(b, raw):
        x_lo = lax.div(b, 2)
        for k in range(4):
            for half in range(2):
                c_copy(x_lo, lax.rem(b, 2) * 4 + k, 1 - c, half).wait_recv()
        cols = jnp.concatenate(
            [h[half, pl.ds(b * 8, 8)].reshape(8 * SH, 128) for half in range(2)], axis=1
        )
        part = w[:, pl.ds(pl.multiple_of(b * 8 * SH, 128), 8 * SH)]
        return raw + jnp.dot(part, cols, preferred_element_type=F32)

    def blocks(i, raw):
        return block(lax.rem(q * 2 + i, 4), raw)

    raw = lax.fori_loop(0, 4, blocks, jnp.zeros((V, 256), F32))
    ht_copy = pltpu.make_async_copy(h, ht_ref, o_sem)
    ht_copy.start()

    capped = CAP * jnp.tanh(raw / CAP)
    exponent = jnp.exp(capped)
    s_id, t_id = lax.axis_index("section"), lax.axis_index("tensor")
    ids = (s_id * 32 + t_id) * V + lax.broadcasted_iota(jnp.int32, (V, 256), 0)
    hit = ids == slot_target
    sums = jnp.concatenate(
        [
            jnp.sum(exponent, axis=0, keepdims=True),
            jnp.sum(jnp.where(hit, capped, 0.0), axis=0, keepdims=True),
        ],
        axis=0,
    )

    def exchange(stage, index, where, values):
        tot_tx[stage] = values
        tot_rx[stage, index] = values
        for d in FAR:
            rcopy(tot_tx.at[stage], tot_rx.at[stage, index], t_s.at[stage, d], t_r.at[stage, index], where(lax.rem(index + d, 8))).start()
        for d in FAR:
            j = lax.rem(index + d, 8)
            rcopy(tot_tx.at[stage], tot_rx.at[stage, j], t_s.at[stage, d], t_r.at[stage, j], where(j)).wait()
        total = tot_rx[stage, 0]
        for j in range(1, 8):
            total = total + tot_rx[stage, j]
        return total

    sums = exchange(0, x * 2 + c, lambda j: dev(lax.div(j, 2), y, z, lax.rem(j, 2)), sums)
    sums = exchange(1, y, lambda j: dev(x, j, z, c), sums)
    sums = exchange(2, z, lambda j: dev(x, y, j, c), sums)
    total, target_logit = sums[0:1], sums[1:2]

    bend = slot_grad * (1.0 - jnp.square(capped / CAP))
    prob = exponent / total
    logit_grad = (bend * (hit.astype(F32) - prob)).astype(BF16)

    def partial(t):
        rows = wt[pl.ds(pl.multiple_of(t * SH, 16), SH), :]
        return jnp.dot(rows, logit_grad, preferred_element_type=F32)

    def to_core(i):
        return rcopy(ctx.at[i], crx.at[i], c_s.at[i], c_r.at[i], partner)

    def send_core(i, _):
        i = lax.rem(other * 8 + i, 16)
        ctx[i] = partial(i * 2 + 1 - c).astype(BF16)
        to_core(i).start()
        return 0

    lax.fori_loop(0, 16, send_core, 0)

    def own_part(i, _):
        own[i] = partial(i * 2 + c)
        return 0

    lax.fori_loop(0, 16, own_part, 0)

    def to_x(yy, half):
        return rcopy(xtx.at[half, yy], xrx.at[half, yy], x_s.at[half, yy], x_r.at[half, yy], dev(x + 1 - 2 * half, y, z, c))

    def to_z(yy):
        return rcopy(ztx.at[yy], zrx.at[yy], z_s.at[yy], z_r.at[yy], dev(x, y, z + 1 - 2 * lax.rem(yy, 2), c))

    def to_y(frm, to):
        return rcopy(ytx.at[to], yrx.at[frm], y_s.at[to], y_r.at[frm], dev(x, to, z, c))

    def send_x(yy, _):
        i = other * 8 + yy
        to_core(i).wait_recv()
        both = own[i] + crx[i].astype(F32)
        for half in range(2):
            xtx[half, yy] = both[:, half * 128 : (half + 1) * 128].astype(BF16)
            to_x(yy, half).start()
        return 0

    lax.fori_loop(0, 8, send_x, 0)

    first = p == 0

    def send_z(k, _):
        yy = lax.rem(y + k, 8)
        i = q * 8 + yy
        to_core(i).wait_recv()
        to_x(yy, 0).wait_recv()
        to_x(yy, 1).wait_recv()
        both = own[i] + crx[i].astype(F32)
        low = both[:, 0:128] + xrx[0, yy].astype(F32)
        high = both[:, 128:256] + xrx[1, yy].astype(F32)
        ztx[yy] = jnp.where(first, high, low).astype(BF16)
        to_z(yy).start()
        own[i, :, 0:128] = jnp.where(first, low, high)
        return 0

    lax.fori_loop(0, 8, send_z, 0)

    def send_y(k, _):
        yy = lax.rem(y + k, 8)
        to_z(yy).wait_recv()
        ytx[yy] = (own[q * 8 + yy, :, 0:128] + zrx[yy].astype(F32)).astype(BF16)
        to_y(y, yy).start()
        return 0

    lax.fori_loop(1, 8, send_y, 0)
    to_z(y).wait_recv()
    acc = own[q * 8 + y, :, 0:128] + zrx[y].astype(F32)
    soft_ref[...] = (-(slot_grad * prob) * (1.0 - jnp.square(capped / CAP))).astype(BF16)
    for d in NEAR:
        yy = at_y(d)
        to_y(yy, y).wait_recv()
        acc = acc + yrx[yy].astype(F32)

    def member(j):
        return dev(2 * lax.rem(j, 2) + q, y, 2 * lax.div(j, 2) + p, c)

    index = zq * 2 + x_hi
    for j in range(8):
        rtx[j, 0:16] = acc[16 * j : 16 * j + 16].astype(BF16)
        rtx[j, 16:32] = acc[128:144].astype(BF16)

    def to_member(frm, to):
        return rcopy(rtx.at[to], rrx.at[frm], r_s.at[to], r_r.at[frm], member(to))

    for d in FAR:
        to_member(index, lax.rem(index + d, 8)).start()
    rrx[index] = rtx[index]
    for d in FAR:
        to_member(lax.rem(index + d, 8), index).wait_recv()
    done = rrx[0].astype(F32)
    for j in range(1, 8):
        done = done + rrx[j].astype(F32)
    atx[...] = done.astype(BF16)

    z2 = z + 1 - 2 * p
    slot = pl.ds(pl.multiple_of(index * 16, 16), 16)
    tail = pl.ds(128, 16)
    arx[p, slot] = atx[0:16]
    arx[p, tail] = atx[16:32]
    tail_copy = rcopy(atx.at[pl.ds(16, 16)], arx.at[p, tail], b_s, b_r, dev(x, y, z2, c))
    tail_copy.start()
    mates = [(a, d) for d in FAR + (0,) for a in range(2) if a or d]

    def to_mate(n, a, d):
        return rcopy(atx.at[pl.ds(0, 16)], arx.at[p, slot], a_s.at[n], a_r.at[n], dev(x + 2 * a, y, z + d, c))

    def from_mate(n, a, d):
        zz = lax.rem(z - d + 8, 8)
        pp = lax.rem(zz, 2)
        ii = lax.div(zz, 2) * 2 + lax.rem(x_hi + a, 2)
        there = pl.ds(pl.multiple_of(ii * 16, 16), 16)
        return rcopy(atx.at[pl.ds(0, 16)], arx.at[pp, there], a_s.at[n], a_r.at[n], dev(x + 2 * a, y, z - d, c))

    for n, (a, d) in enumerate(mates):
        to_mate(n, a, d).start()

    logprob = target_logit - jnp.log(total)
    scale = slot_grad * (1.0 - jnp.square(target_logit / CAP))
    stat_ref[...] = jnp.concatenate([logprob, scale], axis=0)

    for d in FAR:
        y_copy(y, at_y(d)).wait_send()
    for d in NEAR:
        z_copy(at_y(d), p).wait_send()
    for d in (0,) + NEAR:
        for half in range(2):
            x_copy(q, at_y(d), half).wait_send()
            for x_lo in range(2):
                c_copy(x_lo, at_y(d), c, half).wait_send()

    def drain(yy, _):
        to_core(yy).wait_send()
        to_core(yy + 8).wait_send()
        to_x(yy, 0).wait_send()
        to_x(yy, 1).wait_send()
        to_z(yy).wait_send()
        return 0

    lax.fori_loop(0, 8, drain, 0)
    for d in FAR:
        to_y(y, at_y(d)).wait_send()
        to_member(index, lax.rem(index + d, 8)).wait_send()
    ht_copy.wait()
    for n, (a, d) in enumerate(mates):
        from_mate(n, a, d).wait_recv()
        to_mate(n, a, d).wait_send()
    rcopy(atx.at[pl.ds(16, 16)], arx.at[1 - p, tail], b_s, b_r, dev(x, y, z2, c)).wait()
    hg_ref[...] = arx[...]


def finish_kernel(ht_ref, soft_ref, hg_ref, stat_ref, plan_ref, weight_grad_ref, hidden_grad_ref, logprob_ref, scale_ref):
    cols = jnp.concatenate([ht_ref[0], ht_ref[1]], axis=1)
    weight_grad_ref[...] = lax.dot_general(
        soft_ref[...], cols, (((1,), (1,)), ((), ())), preferred_element_type=F32
    ).astype(BF16)

    @pl.when(pl.program_id(0) == 0)
    def _():
        for half in range(2):
            grad = hg_ref[half].astype(F32)
            flat = jnp.transpose(jnp.concatenate([grad, jnp.zeros((112, 128), F32)], axis=0), (1, 0))
            for k in range(2):
                hidden_grad_ref[half * 2 + k] = flat[k * SLOT : k * SLOT + ROWS, 0:SH].astype(BF16)
        for row, out in enumerate((logprob_ref, scale_ref)):
            for m in range(MICRO):
                value = jnp.zeros((1, ROWS), F32)
                for k in range(MICRO):
                    value = jnp.where(plan_ref[k] == m, stat_ref[row : row + 1, k * SLOT : k * SLOT + ROWS], value)
                out[m : m + 1, :] = value


def per_device(hidden, weight, targets, plan, row_grad):
    vmem = pl.BlockSpec(memory_space=pltpu.VMEM)
    smem = pl.BlockSpec(memory_space=pltpu.SMEM)
    hbm = pl.BlockSpec(memory_space=pl.ANY)
    dma = pltpu.SemaphoreType.DMA
    piece = (SH, 128)
    targets = jnp.pad(targets, ((0, 0), (0, SLOT - ROWS)))
    row_grad = jnp.pad(row_grad, ((0, 0), (0, SLOT - ROWS)))
    ht, soft, hg, stat = pl.pallas_call(
        comm_kernel,
        out_shape=(
            jax.ShapeDtypeStruct((2, 32) + piece, BF16),
            jax.ShapeDtypeStruct((V, 256), BF16),
            jax.ShapeDtypeStruct((2,) + piece, BF16),
            jax.ShapeDtypeStruct((2, 256), F32),
        ),
        in_specs=[vmem, hbm, vmem, smem, vmem],
        out_specs=(hbm, vmem, vmem, vmem),
        scratch_shapes=[
            pltpu.VMEM((256, 256), F32),
            pltpu.VMEM((2, 32) + piece, BF16),
            pltpu.VMEM((V, D), BF16),
            pltpu.VMEM((D, V), BF16),
            pltpu.VMEM((16, SH, 256), F32),
            pltpu.VMEM((16, SH, 256), BF16),
            pltpu.VMEM((16, SH, 256), BF16),
            pltpu.VMEM((2, 8) + piece, BF16),
            pltpu.VMEM((2, 8) + piece, BF16),
            pltpu.VMEM((8,) + piece, BF16),
            pltpu.VMEM((8,) + piece, BF16),
            pltpu.VMEM((8,) + piece, BF16),
            pltpu.VMEM((8,) + piece, BF16),
            pltpu.VMEM((8, 32, 128), BF16),
            pltpu.VMEM((8, 32, 128), BF16),
            pltpu.VMEM((32, 128), BF16),
            pltpu.VMEM((2,) + piece, BF16),
            pltpu.VMEM((3, 2, 256), F32),
            pltpu.VMEM((3, 8, 2, 256), F32),
            dma, dma,
            dma((8,)), dma((8,)), dma((8,)), dma((8,)), dma((2, 8)), dma((2, 8)), dma((2, 16)), dma((2, 16)),
            dma((3, 8)), dma((3, 8)), dma((16,)), dma((16,)), dma((2, 8)), dma((2, 8)), dma((8,)), dma((8,)),
            dma((8,)), dma((8,)), dma((8,)), dma((8,)), dma((15,)), dma((15,)), dma, dma,
        ],
        compiler_params=pltpu.CompilerParams(collective_id=0, has_side_effects=True, vmem_limit_bytes=44 << 20),
        name="gather_logits_reduce",
    )(hidden, weight, targets, plan, row_grad)
    chunk = 1152
    weight_grad, hidden_grad, logprob, scale = pl.pallas_call(
        finish_kernel,
        grid=(D // chunk,),
        out_shape=(
            jax.ShapeDtypeStruct((V, D), BF16),
            jax.ShapeDtypeStruct((MICRO, ROWS, SH), BF16),
            jax.ShapeDtypeStruct((MICRO, ROWS), F32),
            jax.ShapeDtypeStruct((MICRO, ROWS), F32),
        ),
        in_specs=[
            pl.BlockSpec((2, chunk, 128), lambda i: (0, i, 0)),
            pl.BlockSpec((V, 256), lambda i: (0, 0)),
            pl.BlockSpec((2,) + piece, lambda i: (0, 0, 0)),
            pl.BlockSpec((2, 256), lambda i: (0, 0)),
            smem,
        ],
        out_specs=(
            pl.BlockSpec((V, chunk), lambda i: (0, i)),
            pl.BlockSpec((MICRO, ROWS, SH), lambda i: (0, 0, 0)),
            pl.BlockSpec((MICRO, ROWS), lambda i: (0, 0)),
            pl.BlockSpec((MICRO, ROWS), lambda i: (0, 0)),
        ),
        compiler_params=pltpu.CompilerParams(vmem_limit_bytes=32 << 20),
        name="weight_gradient",
    )(ht.reshape(2, D, 128), soft, hg, stat, plan)
    return logprob, hidden_grad, weight_grad, scale


def solution(mesh):
    placed = (P(None, None, "tensor"), P(("section", "tensor"), None), P(), P(), P())
    return jax.shard_map(
        per_device,
        mesh=mesh,
        in_specs=placed,
        out_specs=(P(), P(None, None, "tensor"), P(("section", "tensor"), None), P()),
        check_vma=False,
    )
```

time: 429 us -> 97 us (0.23)
  the two profiles are of different devices: /device:TPU:2 before, /device:TPU:16 now
where the time goes in v1:
time: 97 us; the launch traced here: 96.8 us
  Pallas kernels  90.8 us (94%)
  local copies, waits for them, and re-layouts  5.32 us (5%)
    pallas_call x1, Pallas kernels, per_device(): pl.pallas_call(comm_kernel, out_shape=(jax.ShapeDtypeStruct((2, 32) + pie...  87 us
    unnamed x6, local copies, waits for them, and re-layouts  3.95 us
    pallas_call x1, Pallas kernels, per_device(): pl.pallas_call(finish_kernel, grid=(D // chunk,), out_shape=(jax.ShapeDty...  3.78 us

profile of v1, /device:TPU:16, one launch (start us, length us, event | category | flops | bytes accessed | tf_op | source)
XLA Modules:
  0.0 96.8 jit_solution(15763144288498400663)
XLA Ops:
  0.6 0.7 pad.8.targets_ref
  1.3 0.7 pad.9.grad_ref
  2.0 0.9 copy.9.hidden_ref
  2.9 0.0 copy-start
  2.9 1.7 %copy-done = bf16[272,4608]{1,0:T(8,128)(2,1)S(1)} copy-done((bf16[272,4608]{1,0:T(8,128)(2,1)S(1)}, bf16[272,4608]{1,0:T(8,128)(2,1)}, u32[]{:S(2)}) %copy-start) | copy-done | bytes 2506776
  4.6 0.0 copy-start.1
  4.6 0.7 copy-done.1
  5.3 87.0 %gather_logits_reduce.1 = (bf16[2,32,144,128]{3,2,1,0:T(8,128)(2,1)S(1)}, bf16[272,256]{1,0:T(8,128)(2,1)S(1)}, bf16[2,144,128]{2,1,0:T(8,128)(2,1)S(1)}, f32[2,256]{1,0:T(2,128)S(1)}) custom-call(bf16[4,52,144]{2,1,0:T(8,128)(2,1)S(1)} %copy.9.hidden_ref, bf16[272,4608]{1,0:T(8,128)(2,1)S(1)} %copy-done, s32[4,64]{1,0:T(4,128)S(1)} %pad.8.targets_ref, ...), custom_call_target="tpu_custom_call" | custom-call | tf_op jit(solution)/shard_map/gather_logits_reduce/pallas_call | solution.py:370
  92.3 3.8 %weight_gradient.1 = (bf16[272,4608]{1,0:T(8,128)(2,1)}, bf16[4,52,144]{2,1,0:T(8,128)(2,1)S(1)}, f32[4,52]{1,0:T(4,128)}, f32[4,52]{1,0:T(4,128)}) custom-call(bf16[2,4608,128]{2,1,0:T(8,128)(2,1)S(1)} %bitcast.1, bf16[272,256]{1,0:T(8,128)(2,1)S(1)} %get-tuple-element.13.soft_ref, bf16[2,144,128]{2,1,0:T(8,128)(2,1)S(1)} %get-tuple-element.14.hg_ref, ...), custom_call_target="tpu_custom_call" | custom-call | tf_op jit(solution)/shard_map/weight_gradient/pallas_call | solution.py:409
  96.1 0.7 copy.10
Async XLA Ops:
  2.9 1.7 %copy-start = (bf16[272,4608]{1,0:T(8,128)(2,1)S(1)}, bf16[272,4608]{1,0:T(8,128)(2,1)}, u32[]{:S(2)}) copy-start(bf16[272,4608]{1,0:T(8,128)(2,1)} %weight_ref.1) | copy-start | bytes 7520260
  4.6 0.7 copy-start.1

commit v2 on v1

v2 whole, which is shorter than its diff:
```python
import functools

import jax
import jax.numpy as jnp
from jax import lax
from jax.experimental import pallas as pl
from jax.experimental.pallas import tpu as pltpu
from jax.sharding import PartitionSpec as P

MESH = pl.DeviceIdType.MESH
CAP = 30.0
F32 = jnp.float32
BF16 = jnp.bfloat16
MICRO = 4
ROWS = 52
SLOT = 64
V = 272
D = 4608
SH = 144
NEAR = (1, 7, 2, 6, 3, 5, 4)
FAR = (4, 3, 5, 2, 6, 1, 7)


def coords():
    s = lax.axis_index("section")
    t = lax.axis_index("tensor")
    x_hi, z = lax.rem(s, 2), lax.div(s, 2)
    q, y, c = lax.div(t, 16), lax.rem(lax.div(t, 2), 8), lax.rem(t, 2)
    return x_hi * 2 + q, y, z, c


def dev(x, y, z, c):
    x, y, z, c = lax.rem(x + 4, 4), lax.rem(y + 8, 8), lax.rem(z + 8, 8), lax.rem(c + 2, 2)
    return (z * 2 + lax.div(x, 2), lax.rem(x, 2) * 16 + y * 2 + c)


def rcopy(src, dst, ss, rs, to):
    return pltpu.make_async_remote_copy(
        src_ref=src, dst_ref=dst, send_sem=ss, recv_sem=rs, device_id=to, device_id_type=MESH
    )


def slot_lanes(ref, wide, plan_ref, fill, dtype):
    wide[...] = jnp.zeros_like(wide)
    wide[:, 0:ROWS] = ref[...]
    parts = []
    for k in range(MICRO):
        row = jnp.zeros((1, SLOT), dtype)
        for j in range(MICRO):
            row = jnp.where(plan_ref[k] == j, wide[j : j + 1, 0:SLOT], row)
        parts.append(row)
    flat = jnp.concatenate(parts, axis=1)
    lane = lax.broadcasted_iota(jnp.int32, (1, 4 * SLOT), 1)
    return jnp.where(lax.rem(lane, SLOT) < ROWS, flat, jnp.full_like(flat, fill))


def comm_kernel(
    hidden_ref, weight_ref, targets_ref, plan_ref, grad_ref,
    weight_grad_ref, hidden_grad_ref, logprob_ref, scale_ref,
    hid, tgt, grd, pln, tgt_wide, grd_wide, spread, pad, h, w, wt, wg,
    own, ctx, crx, xtx, xrx, ztx, zrx, own_t, ctx_t, crx_t, xtx_t, xrx_t, ztx_t, zrx_t,
    ytx, yrx, rtx, rrx, atx, arx, tot_tx, tot_rx,
    in_sem, o_sem,
    gy_s, gy_r, gz_s, gz_r, gx_s, gx_r, gc_s, gc_r,
    t_s, t_r, c_s, c_r, x_s, x_r, z_s, z_r, ct_s, ct_r, xt_s, xt_r, zt_s, zt_r,
    y_s, y_r, r_s, r_r, a_s, a_r, b_s, b_r,
):
    x, y, z, c = coords()
    q, x_hi, p, zq = lax.rem(x, 2), lax.div(x, 2), lax.rem(z, 2), lax.div(z, 2)
    other = 1 - q
    first = p == 0
    me = q * 16 + y * 2 + c
    partner = dev(x, y, z, 1 - c)

    barrier = pltpu.get_barrier_semaphore()
    peers = [dev(x, y + d, z, c) for d in range(1, 8)]
    peers += [dev(x + a, y, z, c + b) for a in range(4) for b in range(2) if a or b]
    peers += [dev(x + 2 * a, y, z + d, c) for d in range(1, 8) for a in range(2)]
    loads = [
        pltpu.make_async_copy(src, dst, in_sem.at[i])
        for i, (src, dst) in enumerate(
            ((hidden_ref, hid), (plan_ref, pln), (targets_ref, tgt), (grad_ref, grd), (weight_ref, w))
        )
    ]
    for load in loads:
        load.start()
    for peer in peers:
        pl.semaphore_signal(barrier, inc=1, device_id=peer, device_id_type=MESH)

    for load in loads[:4]:
        load.wait()
    spread[...] = hid[...].astype(F32)
    pad[...] = jnp.zeros_like(pad)
    for k in range(MICRO):
        pad[k * SLOT : k * SLOT + ROWS, 0:SH] = spread[:, k, :]
    mine = jnp.transpose(pad[...], (1, 0))[0:SH]
    h[0, me] = mine[:, 0:128].astype(BF16)
    h[1, me] = mine[:, 128:256].astype(BF16)
    slot_target = slot_lanes(tgt, tgt_wide, pln, -1, jnp.int32)
    slot_grad = slot_lanes(grd, grd_wide, pln, 0.0, F32)
    s_id, t_id = lax.axis_index("section"), lax.axis_index("tensor")
    ids = (s_id * 32 + t_id) * V + lax.broadcasted_iota(jnp.int32, (V, 256), 0)
    hit = ids == slot_target
    hot = hit.astype(F32).astype(BF16)

    loads[4].wait()
    for j in range(D // 128):
        wt[j * 128 : (j + 1) * 128, :] = jnp.transpose(w[:, j * 128 : (j + 1) * 128], (1, 0))

    def partial(t, terms):
        rows = wt[pl.ds(pl.multiple_of(t * SH, 16), SH), :]
        return jnp.dot(rows, terms, preferred_element_type=F32)

    def target_part(i, _):
        ctx_t[i] = partial(i * 2 + 1 - c, hot).astype(BF16)
        own_t[i] = partial(i * 2 + c, hot).astype(BF16)
        return 0

    lax.fori_loop(0, 16, target_part, 0)
    pl.semaphore_wait(barrier, len(peers))

    def shard(x_lo, yy):
        return x_lo * 16 + yy * 2 + c

    def y_copy(yy, to_y):
        t = shard(q, yy)
        return rcopy(h.at[p, t], h.at[p, t], gy_s.at[to_y], gy_r.at[yy], dev(x, to_y, z, c))

    def z_copy(yy, half):
        t = shard(q, yy)
        return rcopy(h.at[half, t], h.at[half, t], gz_s.at[yy], gz_r.at[yy], dev(x, y, z + 1 - 2 * lax.rem(yy, 2), c))

    def x_copy(x_lo, yy, half):
        t = shard(x_lo, yy)
        return rcopy(h.at[half, t], h.at[half, t], gx_s.at[half, yy], gx_r.at[half, yy], dev(x + 1 - 2 * half, y, z, c))

    def c_copy(x_lo, yy, cc, half):
        t = x_lo * 16 + yy * 2 + cc
        i = x_lo * 8 + yy
        return rcopy(h.at[half, t], h.at[half, t], gc_s.at[half, i], gc_r.at[half, i], partner)

    def to_core(i):
        return rcopy(ctx.at[i], crx.at[i], c_s.at[i], c_r.at[i], partner)

    def to_core_t(i):
        return rcopy(ctx_t.at[i], crx_t.at[i], ct_s.at[i], ct_r.at[i], partner)

    def to_x(yy, half):
        return rcopy(xtx.at[half, yy], xrx.at[half, yy], x_s.at[half, yy], x_r.at[half, yy], dev(x + 1 - 2 * half, y, z, c))

    def to_x_t(yy, half):
        return rcopy(xtx_t.at[half, yy], xrx_t.at[half, yy], xt_s.at[half, yy], xt_r.at[half, yy], dev(x + 1 - 2 * half, y, z, c))

    def to_z(yy):
        return rcopy(ztx.at[yy], zrx.at[yy], z_s.at[yy], z_r.at[yy], dev(x, y, z + 1 - 2 * lax.rem(yy, 2), c))

    def to_z_t(yy):
        return rcopy(ztx_t.at[yy], zrx_t.at[yy], zt_s.at[yy], zt_r.at[yy], dev(x, y, z + 1 - 2 * lax.rem(yy, 2), c))

    def to_y(frm, to):
        return rcopy(ytx.at[to], yrx.at[frm], y_s.at[to], y_r.at[frm], dev(x, to, z, c))

    def at_y(d):
        return lax.rem(y + d, 8)

    def send_x_t(yy, _):
        i = other * 8 + yy
        to_core_t(i).wait_recv()
        both = own_t[i].astype(F32) + crx_t[i].astype(F32)
        for half in range(2):
            xtx_t[half, yy] = both[:, half * 128 : (half + 1) * 128].astype(BF16)
            to_x_t(yy, half).start()
        return 0

    for d in FAR:
        y_copy(y, at_y(d)).start()
    for half in range(2):
        x_copy(q, y, half).start()
        c_copy(q, y, c, half).start()

    def start_core_t(i, _):
        to_core_t(lax.rem(other * 8 + i, 16)).start()
        return 0

    lax.fori_loop(0, 16, start_core_t, 0)
    lax.fori_loop(0, 4, send_x_t, 0)
    for d in NEAR:
        yy = at_y(d)
        y_copy(yy, y).wait_recv()
        z_copy(yy, p).start()
        x_copy(q, yy, p).start()
        c_copy(q, yy, c, p).start()
    for d in NEAR:
        yy = at_y(d)
        z_copy(yy, 1 - p).wait_recv()
        x_copy(q, yy, 1 - p).start()
        c_copy(q, yy, c, 1 - p).start()
    for d in (0,) + NEAR:
        yy = at_y(d)
        for half in range(2):
            x_copy(other, yy, half).wait_recv()
            c_copy(other, yy, c, half).start()
    lax.fori_loop(4, 8, send_x_t, 0)

    def columns(b):
        return jnp.concatenate(
            [h[half, pl.ds(b * 8, 8)].reshape(8 * SH, 128) for half in range(2)], axis=1
        )

    def blocks(i, raw):
        b = lax.rem(q * 2 + i, 4)
        x_lo = lax.div(b, 2)
        for k in range(4):
            for half in range(2):
                c_copy(x_lo, lax.rem(b, 2) * 4 + k, 1 - c, half).wait_recv()
        part = w[:, pl.ds(pl.multiple_of(b * 8 * SH, 128), 8 * SH)]
        return raw + jnp.dot(part, columns(b), preferred_element_type=F32)

    raw = lax.fori_loop(0, 4, blocks, jnp.zeros((V, 256), F32))
    capped = CAP * jnp.tanh(raw / CAP)
    exponent = jnp.exp(capped)
    curve = 1.0 - jnp.square(capped / CAP)
    sums = jnp.concatenate(
        [
            jnp.sum(exponent, axis=0, keepdims=True),
            jnp.sum(jnp.where(hit, capped, 0.0), axis=0, keepdims=True),
        ],
        axis=0,
    )

    def member_of(stage, j):
        if stage == 0:
            return dev(lax.div(j, 2), y, z, lax.rem(j, 2))
        return dev(x, j, z, c) if stage == 1 else dev(x, y, j, c)

    index_of = (x * 2 + c, y, z)

    def tot_copy(stage, frm, d):
        to = member_of(stage, lax.rem(index_of[stage] + d, 8))
        return rcopy(tot_tx.at[stage], tot_rx.at[stage, frm], t_s.at[stage, d], t_r.at[stage, frm], to)

    def begin(stage, values):
        tot_tx[stage] = values
        tot_rx[stage, index_of[stage]] = values
        for d in FAR:
            tot_copy(stage, index_of[stage], d).start()

    def end(stage):
        for d in FAR:
            tot_copy(stage, lax.rem(index_of[stage] + d, 8), d).wait()
        total = tot_rx[stage, 0]
        for j in range(1, 8):
            total = total + tot_rx[stage, j]
        return total

    begin(0, sums)
    terms = jnp.where(hit, 0.0, exponent * curve).astype(BF16)

    def send_core(i, _):
        ctx[i] = partial(i * 2 + 1 - c, terms).astype(BF16)
        to_core(i).start()
        return 0

    def own_part(i, _):
        own[i] = partial(i * 2 + c, terms)
        return 0

    lax.fori_loop(other * 8, other * 8 + 8, send_core, 0)
    lax.fori_loop(other * 8, other * 8 + 8, own_part, 0)

    def send_x(yy, _):
        i = other * 8 + yy
        to_core(i).wait_recv()
        both = own[i] + crx[i].astype(F32)
        for half in range(2):
            xtx[half, yy] = both[:, half * 128 : (half + 1) * 128].astype(BF16)
            to_x(yy, half).start()
        return 0

    lax.fori_loop(0, 8, send_x, 0)
    begin(1, end(0))
    lax.fori_loop(q * 8, q * 8 + 8, send_core, 0)
    lax.fori_loop(q * 8, q * 8 + 8, own_part, 0)

    def send_z_t(k, _):
        yy = lax.rem(y + k, 8)
        i = q * 8 + yy
        to_core_t(i).wait_recv()
        to_x_t(yy, 0).wait_recv()
        to_x_t(yy, 1).wait_recv()
        both = own_t[i].astype(F32) + crx_t[i].astype(F32)
        low = both[:, 0:128] + xrx_t[0, yy].astype(F32)
        high = both[:, 128:256] + xrx_t[1, yy].astype(F32)
        ztx_t[yy] = jnp.where(first, high, low).astype(BF16)
        to_z_t(yy).start()
        own_t[i, :, 0:128] = jnp.where(first, low, high).astype(BF16)
        return 0

    lax.fori_loop(0, 8, send_z_t, 0)
    begin(2, end(1))

    def send_z(k, _):
        yy = lax.rem(y + k, 8)
        i = q * 8 + yy
        to_core(i).wait_recv()
        to_x(yy, 0).wait_recv()
        to_x(yy, 1).wait_recv()
        both = own[i] + crx[i].astype(F32)
        low = both[:, 0:128] + xrx[0, yy].astype(F32)
        high = both[:, 128:256] + xrx[1, yy].astype(F32)
        ztx[yy] = jnp.where(first, high, low).astype(BF16)
        to_z(yy).start()
        own[i, :, 0:128] = jnp.where(first, low, high)
        return 0

    lax.fori_loop(0, 8, send_z, 0)
    sums = end(2)
    total, target_logit = sums[0:1], sums[1:2]
    target_curve = 1.0 - jnp.square(target_logit / CAP)
    coef_t = slot_grad * (1.0 - jnp.exp(target_logit) / total) * target_curve
    coef_s = slot_grad / total
    half_t = jnp.where(first, coef_t[:, 0:128], coef_t[:, 128:256])
    half_s = jnp.where(first, coef_s[:, 0:128], coef_s[:, 128:256])

    def merged(yy):
        to_z(yy).wait_recv()
        to_z_t(yy).wait_recv()
        i = q * 8 + yy
        soft_sum = own[i, :, 0:128] + zrx[yy].astype(F32)
        target_sum = own_t[i, :, 0:128].astype(F32) + zrx_t[yy].astype(F32)
        return half_t * target_sum - half_s * soft_sum

    def send_y(k, _):
        yy = lax.rem(y + k, 8)
        ytx[yy] = merged(yy).astype(BF16)
        to_y(y, yy).start()
        return 0

    lax.fori_loop(1, 8, send_y, 0)
    acc = merged(y)

    soft = (-(slot_grad * (exponent / total)) * curve).astype(BF16)

    def grad_block(b, _):
        wg[:, pl.ds(pl.multiple_of(b * 8 * SH, 128), 8 * SH)] = lax.dot_general(
            soft, columns(b), (((1,), (1,)), ((), ())), preferred_element_type=F32
        ).astype(BF16)
        return 0

    lax.fori_loop(0, 4, grad_block, 0)
    wg_copy = pltpu.make_async_copy(wg, weight_grad_ref, o_sem)
    wg_copy.start()
    logprob = target_logit - jnp.log(total)
    scale = slot_grad * target_curve
    for m in range(MICRO):
        for value, out in ((logprob, logprob_ref), (scale, scale_ref)):
            row = jnp.zeros((1, ROWS), F32)
            for k in range(MICRO):
                row = jnp.where(pln[k] == m, value[:, k * SLOT : k * SLOT + ROWS], row)
            out[m : m + 1, :] = row

    for d in NEAR:
        yy = at_y(d)
        to_y(yy, y).wait_recv()
        acc = acc + yrx[yy].astype(F32)

    def member(j):
        return dev(2 * lax.rem(j, 2) + q, y, 2 * lax.div(j, 2) + p, c)

    index = zq * 2 + x_hi
    for j in range(8):
        rtx[j, 0:16] = acc[16 * j : 16 * j + 16].astype(BF16)
        rtx[j, 16:32] = acc[128:144].astype(BF16)

    def to_member(frm, to):
        return rcopy(rtx.at[to], rrx.at[frm], r_s.at[to], r_r.at[frm], member(to))

    for d in FAR:
        to_member(index, lax.rem(index + d, 8)).start()
    rrx[index] = rtx[index]
    for d in FAR:
        to_member(lax.rem(index + d, 8), index).wait_recv()
    done = rrx[0].astype(F32)
    for j in range(1, 8):
        done = done + rrx[j].astype(F32)
    atx[...] = done.astype(BF16)

    z2 = z + 1 - 2 * p
    slot = pl.ds(pl.multiple_of(index * 16, 16), 16)
    tail = pl.ds(128, 16)
    arx[p, slot] = atx[0:16]
    arx[p, tail] = atx[16:32]
    tail_copy = rcopy(atx.at[pl.ds(16, 16)], arx.at[p, tail], b_s, b_r, dev(x, y, z2, c))
    tail_copy.start()
    mates = [(a, d) for d in FAR + (0,) for a in range(2) if a or d]

    def to_mate(n, a, d):
        return rcopy(atx.at[pl.ds(0, 16)], arx.at[p, slot], a_s.at[n], a_r.at[n], dev(x + 2 * a, y, z + d, c))

    def from_mate(n, a, d):
        zz = lax.rem(z - d + 8, 8)
        pp = lax.rem(zz, 2)
        ii = lax.div(zz, 2) * 2 + lax.rem(x_hi + a, 2)
        there = pl.ds(pl.multiple_of(ii * 16, 16), 16)
        return rcopy(atx.at[pl.ds(0, 16)], arx.at[pp, there], a_s.at[n], a_r.at[n], dev(x + 2 * a, y, z - d, c))

    for n, (a, d) in enumerate(mates):
        to_mate(n, a, d).start()

    for d in FAR:
        y_copy(y, at_y(d)).wait_send()
    for d in NEAR:
        z_copy(at_y(d), p).wait_send()
    for d in (0,) + NEAR:
        for half in range(2):
            x_copy(q, at_y(d), half).wait_send()
            for x_lo in range(2):
                c_copy(x_lo, at_y(d), c, half).wait_send()

    def drain(yy, _):
        for base in range(2):
            to_core(yy + 8 * base).wait_send()
            to_core_t(yy + 8 * base).wait_send()
            to_x(yy, base).wait_send()
            to_x_t(yy, base).wait_send()
        to_z(yy).wait_send()
        to_z_t(yy).wait_send()
        return 0

    lax.fori_loop(0, 8, drain, 0)
    for d in FAR:
        to_y(y, at_y(d)).wait_send()
        to_member(index, lax.rem(index + d, 8)).wait_send()
    wg_copy.wait()
    for n, (a, d) in enumerate(mates):
        from_mate(n, a, d).wait_recv()
        to_mate(n, a, d).wait_send()
    rcopy(atx.at[pl.ds(16, 16)], arx.at[1 - p, tail], b_s, b_r, dev(x, y, z2, c)).wait()
    for half in range(2):
        wide = jnp.concatenate([arx[half].astype(F32), jnp.zeros((256 - SH, 128), F32)], axis=0)
        flat = jnp.transpose(wide, (1, 0))
        for k in range(2):
            spread[:, half * 2 + k, :] = flat[k * SLOT : k * SLOT + ROWS, 0:SH]
    hidden_grad_ref[...] = spread[...].astype(BF16)


def hand_on_kernel(a0, a1, a2, a3, b0, b1, b2, b3, v0, v1, v2, v3, sem_in, sem_out):
    cuts = [(0, 64), (64, 64), (128, 64), (192, 80)]
    pieces = [(a0.at[pl.ds(i, n)], v0.at[pl.ds(i, n)], b0.at[pl.ds(i, n)]) for i, n in cuts]
    pieces += [(a1, v1, b1), (a2, v2, b2), (a3, v3, b3)]
    reads = [pltpu.make_async_copy(a, v, sem_in.at[i]) for i, (a, v, b) in enumerate(pieces)]
    writes = [pltpu.make_async_copy(v, b, sem_out.at[i]) for i, (a, v, b) in enumerate(pieces)]
    for read in reads:
        read.start()
    for read, write in zip(reads, writes):
        read.wait()
        write.start()
    for write in writes:
        write.wait()


def per_device(hidden, weight, targets, plan, row_grad):
    vmem = pl.BlockSpec(memory_space=pltpu.VMEM)
    hbm = pl.BlockSpec(memory_space=pl.ANY)
    dma = pltpu.SemaphoreType.DMA
    piece = (SH, 128)
    outs = (
        jax.ShapeDtypeStruct((V, D), BF16),
        jax.ShapeDtypeStruct((ROWS, MICRO, SH), BF16),
        jax.ShapeDtypeStruct((MICRO, ROWS), F32),
        jax.ShapeDtypeStruct((MICRO, ROWS), F32),
    )
    def buf(*shape, dtype=BF16):
        return pltpu.VMEM(shape, dtype)

    results = pl.pallas_call(
        comm_kernel,
        out_shape=outs,
        in_specs=[hbm] * 5,
        out_specs=(hbm, vmem, vmem, vmem),
        scratch_shapes=[
            buf(ROWS, MICRO, SH), buf(MICRO, ROWS, dtype=jnp.int32), buf(MICRO, ROWS, dtype=F32),
            pltpu.SMEM((MICRO,), jnp.int32),
            buf(MICRO, 128, dtype=jnp.int32), buf(MICRO, 128, dtype=F32),
            buf(ROWS, MICRO, SH, dtype=F32), buf(256, 256, dtype=F32),
            buf(2, 32, *piece), buf(V, D), buf(D, V), buf(V, D),
            buf(16, SH, 256, dtype=F32), buf(16, SH, 256), buf(16, SH, 256),
            buf(2, 8, *piece), buf(2, 8, *piece), buf(8, *piece), buf(8, *piece),
            buf(16, SH, 256), buf(16, SH, 256), buf(16, SH, 256),
            buf(2, 8, *piece), buf(2, 8, *piece), buf(8, *piece), buf(8, *piece),
            buf(8, *piece), buf(8, *piece), buf(8, 32, 128), buf(8, 32, 128), buf(32, 128), buf(2, *piece),
            buf(3, 2, 256, dtype=F32), buf(3, 8, 2, 256, dtype=F32),
            dma((5,)), dma,
            dma((8,)), dma((8,)), dma((8,)), dma((8,)), dma((2, 8)), dma((2, 8)), dma((2, 16)), dma((2, 16)),
            dma((3, 8)), dma((3, 8)), dma((16,)), dma((16,)), dma((2, 8)), dma((2, 8)), dma((8,)), dma((8,)),
            dma((16,)), dma((16,)), dma((2, 8)), dma((2, 8)), dma((8,)), dma((8,)),
            dma((8,)), dma((8,)), dma((8,)), dma((8,)), dma((15,)), dma((15,)), dma, dma,
        ],
        compiler_params=pltpu.CompilerParams(collective_id=0, has_side_effects=True, vmem_limit_bytes=62 << 20),
        name="gather_logits_reduce",
    )(jnp.transpose(hidden, (1, 0, 2)), weight, targets, plan, row_grad)
    weight_grad, hidden_grad, logprob, scale = pl.pallas_call(
        hand_on_kernel,
        out_shape=outs,
        in_specs=[hbm] * 4,
        out_specs=(hbm,) * 4,
        scratch_shapes=[pltpu.VMEM(out.shape, out.dtype) for out in outs] + [dma((7,)), dma((7,))],
        compiler_params=pltpu.CompilerParams(vmem_limit_bytes=62 << 20),
        name="hand_on",
    )(*results)
    return logprob, jnp.transpose(hidden_grad, (1, 0, 2)), weight_grad, scale


def solution(mesh):
    placed = (P(None, None, "tensor"), P(("section", "tensor"), None), P(), P(), P())
    return jax.shard_map(
        per_device,
        mesh=mesh,
        in_specs=placed,
        out_specs=(P(), P(None, None, "tensor"), P(("section", "tensor"), None), P()),
        check_vma=False,
    )
```

time: 97 us -> 81.3 us (0.84)
  the two profiles are of different devices: /device:TPU:16 before, /device:TPU:4 now
where the time goes in v2:
time: 81.3 us; the launch traced here: 81.1 us
  Pallas kernels  80.5 us (99%)
    pallas_call x1, Pallas kernels, per_device(): pl.pallas_call(comm_kernel, out_shape=outs, in_specs=[hbm] * 5, out_specs...  77.8 us
    pallas_call x1, Pallas kernels, per_device(): pl.pallas_call(hand_on_kernel, out_shape=outs, in_specs=[hbm] * 4, out_sp...  2.66 us

profile of v2, /device:TPU:4, one launch (start us, length us, event | category | flops | bytes accessed | tf_op | source)
XLA Modules:
  0.0 81.1 jit_solution(17242678182988160930)
XLA Ops:
  0.6 77.8 %gather_logits_reduce.1 = (bf16[272,4608]{1,0:T(8,128)(2,1)}, bf16[52,4,144]{2,1,0:T(4,128)(2,1)}, f32[4,52]{1,0:T(4,128)}, f32[4,52]{1,0:T(4,128)}) custom-call(bf16[52,4,144]{2,1,0:T(4,128)(2,1)} %bitcast.2, bf16[272,4608]{1,0:T(8,128)(2,1)} %weight_ref.1, s32[4,52]{1,0:T(4,128)} %targets_ref.1, s32[4]{0:T(128)} %plan_ref.1, f32[4,52]{1,0:T(4,128)} %grad_ref.1), custom_call_target="tpu_custom_call" | custom-call | tf_op jit(solution)/shard_map/gather_logits_reduce/pallas_call | solution.py:476
  78.4 2.7 %hand_on.1 = (bf16[272,4608]{1,0:T(8,128)(2,1)}, bf16[52,4,144]{2,1,0:T(4,128)(2,1)}, f32[4,52]{1,0:T(4,128)}, f32[4,52]{1,0:T(4,128)}) custom-call(bf16[272,4608]{1,0:T(8,128)(2,1)} %get-tuple-element.12.a0, bf16[52,4,144]{2,1,0:T(4,128)(2,1)} %get-tuple-element.13.a1, f32[4,52]{1,0:T(4,128)} %get-tuple-element.14.a2, f32[4,52]{1,0:T(4,128)} %get-tuple-element.15.a3), custom_call_target="tpu_custom_call" | custom-call | tf_op jit(solution)/shard_map/hand_on/pallas_call | solution.py:502

commit v3 on v2

--- a/solution.py
+++ b/solution.py
@@ -57,12 +57,12 @@
 def comm_kernel(
     hidden_ref, weight_ref, targets_ref, plan_ref, grad_ref,
     weight_grad_ref, hidden_grad_ref, logprob_ref, scale_ref,
-    hid, tgt, grd, pln, tgt_wide, grd_wide, spread, pad, h, w, wt, wg,
-    own, ctx, crx, xtx, xrx, ztx, zrx, own_t, ctx_t, crx_t, xtx_t, xrx_t, ztx_t, zrx_t,
+    hid, tgt, grd, pln, tgt_wide, grd_wide, spread, pad, h, w, wt, wt_in, wg, term, term_in, hot, hot_in,
+    own, xtx, xrx, ztx, zrx, own_t, xtx_t, xrx_t, ztx_t, zrx_t,
     ytx, yrx, rtx, rrx, atx, arx, tot_tx, tot_rx,
     in_sem, o_sem,
     gy_s, gy_r, gz_s, gz_r, gx_s, gx_r, gc_s, gc_r,
-    t_s, t_r, c_s, c_r, x_s, x_r, z_s, z_r, ct_s, ct_r, xt_s, xt_r, zt_s, zt_r,
+    t_s, t_r, w_s, w_r, m_s, m_r, x_s, x_r, z_s, z_r, xt_s, xt_r, zt_s, zt_r,
     y_s, y_r, r_s, r_r, a_s, a_r, b_s, b_r,
 ):
     x, y, z, c = coords()
@@ -87,37 +87,18 @@
     for peer in peers:
         pl.semaphore_signal(barrier, inc=1, device_id=peer, device_id_type=MESH)
 
-    for load in loads[:4]:
-        load.wait()
+    pad[...] = jnp.zeros_like(pad)
+    loads[0].wait()
     spread[...] = hid[...].astype(F32)
-    pad[...] = jnp.zeros_like(pad)
     for k in range(MICRO):
         pad[k * SLOT : k * SLOT + ROWS, 0:SH] = spread[:, k, :]
     mine = jnp.transpose(pad[...], (1, 0))[0:SH]
     h[0, me] = mine[:, 0:128].astype(BF16)
     h[1, me] = mine[:, 128:256].astype(BF16)
-    slot_target = slot_lanes(tgt, tgt_wide, pln, -1, jnp.int32)
-    slot_grad = slot_lanes(grd, grd_wide, pln, 0.0, F32)
-    s_id, t_id = lax.axis_index("section"), lax.axis_index("tensor")
-    ids = (s_id * 32 + t_id) * V + lax.broadcasted_iota(jnp.int32, (V, 256), 0)
-    hit = ids == slot_target
-    hot = hit.astype(F32).astype(BF16)
-
-    loads[4].wait()
-    for j in range(D // 128):
-        wt[j * 128 : (j + 1) * 128, :] = jnp.transpose(w[:, j * 128 : (j + 1) * 128], (1, 0))
-
-    def partial(t, terms):
-        rows = wt[pl.ds(pl.multiple_of(t * SH, 16), SH), :]
-        return jnp.dot(rows, terms, preferred_element_type=F32)
-
-    def target_part(i, _):
-        ctx_t[i] = partial(i * 2 + 1 - c, hot).astype(BF16)
-        own_t[i] = partial(i * 2 + c, hot).astype(BF16)
-        return 0
-
-    lax.fori_loop(0, 16, target_part, 0)
     pl.semaphore_wait(barrier, len(peers))
+
+    def along(i):
+        return 1 - 2 * lax.rem(i, 2)
 
     def shard(x_lo, yy):
         return x_lo * 16 + yy * 2 + c
@@ -128,34 +109,36 @@
 
     def z_copy(yy, half):
         t = shard(q, yy)
-        return rcopy(h.at[half, t], h.at[half, t], gz_s.at[yy], gz_r.at[yy], dev(x, y, z + 1 - 2 * lax.rem(yy, 2), c))
+        return rcopy(h.at[half, t], h.at[half, t], gz_s.at[yy], gz_r.at[yy], dev(x, y, z + along(yy), c))
 
     def x_copy(x_lo, yy, half):
         t = shard(x_lo, yy)
-        return rcopy(h.at[half, t], h.at[half, t], gx_s.at[half, yy], gx_r.at[half, yy], dev(x + 1 - 2 * half, y, z, c))
+        return rcopy(h.at[half, t], h.at[half, t], gx_s.at[half, yy], gx_r.at[half, yy], dev(x + along(yy), y, z, c))
 
     def c_copy(x_lo, yy, cc, half):
         t = x_lo * 16 + yy * 2 + cc
         i = x_lo * 8 + yy
         return rcopy(h.at[half, t], h.at[half, t], gc_s.at[half, i], gc_r.at[half, i], partner)
 
-    def to_core(i):
-        return rcopy(ctx.at[i], crx.at[i], c_s.at[i], c_r.at[i], partner)
-
-    def to_core_t(i):
-        return rcopy(ctx_t.at[i], crx_t.at[i], ct_s.at[i], ct_r.at[i], partner)
-
-    def to_x(yy, half):
-        return rcopy(xtx.at[half, yy], xrx.at[half, yy], x_s.at[half, yy], x_r.at[half, yy], dev(x + 1 - 2 * half, y, z, c))
-
-    def to_x_t(yy, half):
-        return rcopy(xtx_t.at[half, yy], xrx_t.at[half, yy], xt_s.at[half, yy], xt_r.at[half, yy], dev(x + 1 - 2 * half, y, z, c))
-
-    def to_z(yy):
-        return rcopy(ztx.at[yy], zrx.at[yy], z_s.at[yy], z_r.at[yy], dev(x, y, z + 1 - 2 * lax.rem(yy, 2), c))
-
-    def to_z_t(yy):
-        return rcopy(ztx_t.at[yy], zrx_t.at[yy], zt_s.at[yy], zt_r.at[yy], dev(x, y, z + 1 - 2 * lax.rem(yy, 2), c))
+    def rows_of(i, cc):
+        return pl.ds(pl.multiple_of((i * 2 + cc) * SH, 16), SH)
+
+    def w_copy(i):
+        return rcopy(wt.at[rows_of(i, 1 - c)], wt_in.at[i], w_s.at[i], w_r.at[i], partner)
+
+    term_copy = rcopy(term, term_in, m_s, m_r, partner)
+
+    def to_x(half, yy, way):
+        return rcopy(xtx.at[half, yy], xrx.at[half, yy], x_s.at[half, yy], x_r.at[half, yy], dev(x + way, y, z, c))
+
+    def to_z(x_lo, yy):
+        return rcopy(ztx.at[x_lo, yy], zrx.at[x_lo, yy], z_s.at[x_lo, yy], z_r.at[x_lo, yy], dev(x, y, z + along(yy), c))
+
+    def to_x_t(yy):
+        return rcopy(xtx_t.at[yy], xrx_t.at[yy], xt_s.at[yy], xt_r.at[yy], dev(x + along(yy), y, z, c))
+
+    def to_z_t(x_lo, yy):
+        return rcopy(ztx_t.at[x_lo, yy], zrx_t.at[x_lo, yy], zt_s.at[x_lo, yy], zt_r.at[x_lo, yy], dev(x, y, z + along(yy), c))
 
     def to_y(frm, to):
         return rcopy(ytx.at[to], yrx.at[frm], y_s.at[to], y_r.at[frm], dev(x, to, z, c))
@@ -163,44 +146,83 @@
     def at_y(d):
         return lax.rem(y + d, 8)
 
-    def send_x_t(yy, _):
-        i = other * 8 + yy
-        to_core_t(i).wait_recv()
-        both = own_t[i].astype(F32) + crx_t[i].astype(F32)
-        for half in range(2):
-            xtx_t[half, yy] = both[:, half * 128 : (half + 1) * 128].astype(BF16)
-            to_x_t(yy, half).start()
-        return 0
-
-    for d in FAR:
+    def part_a(k):
+        return lax.div(k, 2) * 4 + lax.rem(k, 2)
+
+    def part_b(k):
+        return part_a(k) + 2
+
+    def halves(value):
+        low, high = value[:, 0:128], value[:, 128:256]
+        return jnp.where(first, low, high), jnp.where(first, high, low)
+
+    def from_mine(i, ref):
+        return jnp.dot(wt[rows_of(i, c), :], ref[...], preferred_element_type=F32)
+
+    def from_theirs(i, ref):
+        return jnp.dot(wt_in[i], ref[...], preferred_element_type=F32)
+
+    for d in NEAR:
         y_copy(y, at_y(d)).start()
     for half in range(2):
         x_copy(q, y, half).start()
         c_copy(q, y, c, half).start()
 
-    def start_core_t(i, _):
-        to_core_t(lax.rem(other * 8 + i, 16)).start()
-        return 0
-
-    lax.fori_loop(0, 16, start_core_t, 0)
-    lax.fori_loop(0, 4, send_x_t, 0)
-    for d in NEAR:
+    loads[4].wait()
+    for j in range(D // 128):
+        wt[j * 128 : (j + 1) * 128, :] = jnp.transpose(w[:, j * 128 : (j + 1) * 128], (1, 0))
+
+    def start_w(i, _):
+        w_copy(i).start()
+        return 0
+
+    lax.fori_loop(0, 16, start_w, 0)
+    for load in loads[1:4]:
+        load.wait()
+    slot_target = slot_lanes(tgt, tgt_wide, pln, -1, jnp.int32)
+    slot_grad = slot_lanes(grd, grd_wide, pln, 0.0, F32)
+    s_id, t_id = lax.axis_index("section"), lax.axis_index("tensor")
+    entry = lax.broadcasted_iota(jnp.int32, (V, 256), 0)
+    hit = (s_id * 32 + t_id) * V + entry == slot_target
+    hot[...] = hit.astype(F32).astype(BF16)
+    hot_in[...] = ((s_id * 32 + t_id + 1 - 2 * c) * V + entry == slot_target).astype(F32).astype(BF16)
+
+    def target_mine(i, _):
+        own_t[i] = from_mine(i, hot).astype(BF16)
+        return 0
+
+    def target_rows(i, _):
+        x_lo, yy = lax.div(i, 8), lax.rem(i, 8)
+        w_copy(i).wait_recv()
+        keep, pass_on = halves(own_t[i].astype(F32) + from_theirs(i, hot_in))
+        own_t[i, :, 0:128] = keep.astype(BF16)
+        ztx_t[x_lo, yy] = pass_on.astype(BF16)
+        to_z_t(x_lo, yy).start()
+        return 0
+
+    for n, d in enumerate(NEAR):
         yy = at_y(d)
         y_copy(yy, y).wait_recv()
         z_copy(yy, p).start()
         x_copy(q, yy, p).start()
         c_copy(q, yy, c, p).start()
-    for d in NEAR:
+        if n < 4:
+            lax.fori_loop(4 * n, 4 * n + 4, target_mine, 0)
+    for n, d in enumerate(NEAR):
         yy = at_y(d)
         z_copy(yy, 1 - p).wait_recv()
         x_copy(q, yy, 1 - p).start()
         c_copy(q, yy, c, 1 - p).start()
+        x_copy(other, yy, p).wait_recv()
+        c_copy(other, yy, c, p).start()
+        lax.fori_loop(2 * n, 2 * n + 2, target_rows, 0)
+    x_copy(other, y, p).wait_recv()
+    c_copy(other, y, c, p).start()
     for d in (0,) + NEAR:
         yy = at_y(d)
-        for half in range(2):
-            x_copy(other, yy, half).wait_recv()
-            c_copy(other, yy, c, half).start()
-    lax.fori_loop(4, 8, send_x_t, 0)
+        x_copy(other, yy, 1 - p).wait_recv()
+        c_copy(other, yy, c, 1 - p).start()
+    lax.fori_loop(14, 16, target_rows, 0)
 
     def columns(b):
         return jnp.concatenate(
@@ -254,66 +276,94 @@
         return total
 
     begin(0, sums)
-    terms = jnp.where(hit, 0.0, exponent * curve).astype(BF16)
-
-    def send_core(i, _):
-        ctx[i] = partial(i * 2 + 1 - c, terms).astype(BF16)
-        to_core(i).start()
-        return 0
-
-    def own_part(i, _):
-        own[i] = partial(i * 2 + c, terms)
-        return 0
-
-    lax.fori_loop(other * 8, other * 8 + 8, send_core, 0)
-    lax.fori_loop(other * 8, other * 8 + 8, own_part, 0)
-
-    def send_x(yy, _):
+    term[...] = jnp.where(hit, 0.0, exponent * curve).astype(BF16)
+    term_copy.start()
+
+    def mine_first(k, _):
+        for i in (other * 8 + part_a(k), other * 8 + part_b(k), q * 8 + part_b(k)):
+            own[i] = from_mine(i, term)
+        return 0
+
+    lax.fori_loop(0, 4, mine_first, 0)
+    term_copy.wait_recv()
+
+    def send_first(k, _):
+        ya, yb = part_a(k), part_b(k)
+        value = own[other * 8 + ya] + from_theirs(other * 8 + ya, term_in)
+        for half in range(2):
+            xtx[half, ya] = value[:, half * 128 : (half + 1) * 128].astype(BF16)
+            to_x(half, ya, 1 - 2 * half).start()
+        for x_lo in (other, q):
+            i = x_lo * 8 + yb
+            keep, pass_on = halves(own[i] + from_theirs(i, term_in))
+            ztx[x_lo, yb] = pass_on.astype(BF16)
+            to_z(x_lo, yb).start()
+            own[i, :, 0:128] = keep
+        return 0
+
+    lax.fori_loop(0, 2, send_first, 0)
+    begin(1, end(0))
+    lax.fori_loop(2, 4, send_first, 0)
+
+    def keep_first(k, _):
+        i = q * 8 + part_a(k)
+        own[i] = from_mine(i, term) + from_theirs(i, term_in)
+        return 0
+
+    lax.fori_loop(0, 4, keep_first, 0)
+
+    def send_x_t(yy, _):
+        to_z_t(other, yy).wait_recv()
         i = other * 8 + yy
-        to_core(i).wait_recv()
-        both = own[i] + crx[i].astype(F32)
+        xtx_t[yy] = (own_t[i, :, 0:128].astype(F32) + zrx_t[other, yy].astype(F32)).astype(BF16)
+        to_x_t(yy).start()
+        return 0
+
+    lax.fori_loop(0, 8, send_x_t, 0)
+
+    def send_second(k, _):
+        ya, yb = part_a(k), part_b(k)
+        to_z(other, yb).wait_recv()
+        xtx[0, yb] = (own[other * 8 + yb, :, 0:128] + zrx[other, yb].astype(F32)).astype(BF16)
+        to_x(0, yb, along(yb)).start()
+        i = q * 8 + ya
+        both = own[i]
         for half in range(2):
-            xtx[half, yy] = both[:, half * 128 : (half + 1) * 128].astype(BF16)
-            to_x(yy, half).start()
-        return 0
-
-    lax.fori_loop(0, 8, send_x, 0)
-    begin(1, end(0))
-    lax.fori_loop(q * 8, q * 8 + 8, send_core, 0)
-    lax.fori_loop(q * 8, q * 8 + 8, own_part, 0)
-
-    def send_z_t(k, _):
-        yy = lax.rem(y + k, 8)
+            to_x(half, ya, 1 - 2 * half).wait_recv()
+        both = both + jnp.concatenate([xrx[0, ya], xrx[1, ya]], axis=1).astype(F32)
+        keep, pass_on = halves(both)
+        ztx[0, ya] = pass_on.astype(BF16)
+        to_z(0, ya).start()
+        own[i, :, 0:128] = keep
+        return 0
+
+    lax.fori_loop(0, 2, send_second, 0)
+    begin(2, end(1))
+    lax.fori_loop(2, 4, send_second, 0)
+
+    def ready_a(k, _):
+        i, yy = q * 8 + part_a(k), part_a(k)
+        to_z(0, yy).wait_recv()
+        own[i, :, 0:128] = own[i, :, 0:128] + zrx[0, yy].astype(F32)
+        return 0
+
+    def ready_b(k, _):
+        i, yy = q * 8 + part_b(k), part_b(k)
+        to_z(q, yy).wait_recv()
+        to_x(0, yy, along(yy)).wait_recv()
+        own[i, :, 0:128] = own[i, :, 0:128] + zrx[q, yy].astype(F32) + xrx[0, yy].astype(F32)
+        return 0
+
+    def ready_t(yy, _):
         i = q * 8 + yy
-        to_core_t(i).wait_recv()
-        to_x_t(yy, 0).wait_recv()
-        to_x_t(yy, 1).wait_recv()
-        both = own_t[i].astype(F32) + crx_t[i].astype(F32)
-        low = both[:, 0:128] + xrx_t[0, yy].astype(F32)
-        high = both[:, 128:256] + xrx_t[1, yy].astype(F32)
-        ztx_t[yy] = jnp.where(first, high, low).astype(BF16)
-        to_z_t(yy).start()
-        own_t[i, :, 0:128] = jnp.where(first, low, high).astype(BF16)
-        return 0
-
-    lax.fori_loop(0, 8, send_z_t, 0)
-    begin(2, end(1))
-
-    def send_z(k, _):
-        yy = lax.rem(y + k, 8)
-        i = q * 8 + yy
-        to_core(i).wait_recv()
-        to_x(yy, 0).wait_recv()
-        to_x(yy, 1).wait_recv()
-        both = own[i] + crx[i].astype(F32)
-        low = both[:, 0:128] + xrx[0, yy].astype(F32)
-        high = both[:, 128:256] + xrx[1, yy].astype(F32)
-        ztx[yy] = jnp.where(first, high, low).astype(BF16)
-        to_z(yy).start()
-        own[i, :, 0:128] = jnp.where(first, low, high)
-        return 0
-
-    lax.fori_loop(0, 8, send_z, 0)
+        to_z_t(q, yy).wait_recv()
+        to_x_t(yy).wait_recv()
+        own_t[i, :, 0:128] = (own_t[i, :, 0:128].astype(F32) + zrx_t[q, yy].astype(F32) + xrx_t[yy].astype(F32)).astype(BF16)
+        return 0
+
+    lax.fori_loop(0, 8, ready_t, 0)
+    lax.fori_loop(0, 4, ready_a, 0)
+    lax.fori_loop(0, 4, ready_b, 0)
     sums = end(2)
     total, target_logit = sums[0:1], sums[1:2]
     target_curve = 1.0 - jnp.square(target_logit / CAP)
@@ -323,12 +373,8 @@
     half_s = jnp.where(first, coef_s[:, 0:128], coef_s[:, 128:256])
 
     def merged(yy):
-        to_z(yy).wait_recv()
-        to_z_t(yy).wait_recv()
         i = q * 8 + yy
-        soft_sum = own[i, :, 0:128] + zrx[yy].astype(F32)
-        target_sum = own_t[i, :, 0:128].astype(F32) + zrx_t[yy].astype(F32)
-        return half_t * target_sum - half_s * soft_sum
+        return half_t * own_t[i, :, 0:128].astype(F32) - half_s * own[i, :, 0:128]
 
     def send_y(k, _):
         yy = lax.rem(y + k, 8)
@@ -416,18 +462,26 @@
             x_copy(q, at_y(d), half).wait_send()
             for x_lo in range(2):
                 c_copy(x_lo, at_y(d), c, half).wait_send()
+    term_copy.wait_send()
 
     def drain(yy, _):
-        for base in range(2):
-            to_core(yy + 8 * base).wait_send()
-            to_core_t(yy + 8 * base).wait_send()
-            to_x(yy, base).wait_send()
-            to_x_t(yy, base).wait_send()
-        to_z(yy).wait_send()
-        to_z_t(yy).wait_send()
+        to_x_t(yy).wait_send()
+        for x_lo in range(2):
+            w_copy(x_lo * 8 + yy).wait_send()
+            to_z_t(x_lo, yy).wait_send()
+        return 0
+
+    def drain_ab(k, _):
+        ya, yb = part_a(k), part_b(k)
+        for half in range(2):
+            to_x(half, ya, 1 - 2 * half).wait_send()
+            to_z(half, yb).wait_send()
+        to_z(0, ya).wait_send()
+        to_x(0, yb, along(yb)).wait_send()
         return 0
 
     lax.fori_loop(0, 8, drain, 0)
+    lax.fori_loop(0, 4, drain_ab, 0)
     for d in FAR:
         to_y(y, at_y(d)).wait_send()
         to_member(index, lax.rem(index + d, 8)).wait_send()
@@ -483,17 +537,16 @@
             pltpu.SMEM((MICRO,), jnp.int32),
             buf(MICRO, 128, dtype=jnp.int32), buf(MICRO, 128, dtype=F32),
             buf(ROWS, MICRO, SH, dtype=F32), buf(256, 256, dtype=F32),
-            buf(2, 32, *piece), buf(V, D), buf(D, V), buf(V, D),
-            buf(16, SH, 256, dtype=F32), buf(16, SH, 256), buf(16, SH, 256),
-            buf(2, 8, *piece), buf(2, 8, *piece), buf(8, *piece), buf(8, *piece),
-            buf(16, SH, 256), buf(16, SH, 256), buf(16, SH, 256),
-            buf(2, 8, *piece), buf(2, 8, *piece), buf(8, *piece), buf(8, *piece),
+            buf(2, 32, *piece), buf(V, D), buf(D, V), buf(16, SH, V), buf(V, D),
+            buf(V, 256), buf(V, 256), buf(V, 256), buf(V, 256),
+            buf(16, SH, 256, dtype=F32), buf(2, 8, *piece), buf(2, 8, *piece), buf(2, 8, *piece), buf(2, 8, *piece),
+            buf(16, SH, 256), buf(8, *piece), buf(8, *piece), buf(2, 8, *piece), buf(2, 8, *piece),
             buf(8, *piece), buf(8, *piece), buf(8, 32, 128), buf(8, 32, 128), buf(32, 128), buf(2, *piece),
             buf(3, 2, 256, dtype=F32), buf(3, 8, 2, 256, dtype=F32),
             dma((5,)), dma,
             dma((8,)), dma((8,)), dma((8,)), dma((8,)), dma((2, 8)), dma((2, 8)), dma((2, 16)), dma((2, 16)),
-            dma((3, 8)), dma((3, 8)), dma((16,)), dma((16,)), dma((2, 8)), dma((2, 8)), dma((8,)), dma((8,)),
-            dma((16,)), dma((16,)), dma((2, 8)), dma((2, 8)), dma((8,)), dma((8,)),
+            dma((3, 8)), dma((3, 8)), dma((16,)), dma((16,)), dma, dma,
+            dma((2, 8)), dma((2, 8)), dma((2, 8)), dma((2, 8)), dma((8,)), dma((8,)), dma((2, 8)), dma((2, 8)),
             dma((8,)), dma((8,)), dma((8,)), dma((8,)), dma((15,)), dma((15,)), dma, dma,
         ],
         compiler_params=pltpu.CompilerParams(collective_id=0, has_side_effects=True, vmem_limit_bytes=62 << 20),

time: 81.3 us -> 75 us (0.923)
  the two profiles are of different devices: /device:TPU:4 before, /device:TPU:48 now
where the time goes in v3:
time: 75 us; the launch traced here: 74.8 us
  Pallas kernels  74.2 us (99%)
    pallas_call x1, Pallas kernels, per_device(): pl.pallas_call(comm_kernel, out_shape=outs, in_specs=[hbm] * 5, out_specs...  71.5 us
    pallas_call x1, Pallas kernels, per_device(): pl.pallas_call(hand_on_kernel, out_shape=outs, in_specs=[hbm] * 4, out_sp...  2.66 us

profile of v3, /device:TPU:48, one launch (start us, length us, event | category | flops | bytes accessed | tf_op | source)
XLA Modules:
  0.0 74.8 jit_solution(10194526577714746828)
XLA Ops:
  0.6 71.5 %gather_logits_reduce.1 = (bf16[272,4608]{1,0:T(8,128)(2,1)}, bf16[52,4,144]{2,1,0:T(4,128)(2,1)}, f32[4,52]{1,0:T(4,128)}, f32[4,52]{1,0:T(4,128)}) custom-call(bf16[52,4,144]{2,1,0:T(4,128)(2,1)} %bitcast.2, bf16[272,4608]{1,0:T(8,128)(2,1)} %weight_ref.1, s32[4,52]{1,0:T(4,128)} %targets_ref.1, s32[4]{0:T(128)} %plan_ref.1, f32[4,52]{1,0:T(4,128)} %grad_ref.1), custom_call_target="tpu_custom_call" | custom-call | tf_op jit(solution)/shard_map/gather_logits_reduce/pallas_call | solution.py:530
  72.1 2.7 %hand_on.1 = (bf16[272,4608]{1,0:T(8,128)(2,1)}, bf16[52,4,144]{2,1,0:T(4,128)(2,1)}, f32[4,52]{1,0:T(4,128)}, f32[4,52]{1,0:T(4,128)}) custom-call(bf16[272,4608]{1,0:T(8,128)(2,1)} %get-tuple-element.12.a0, bf16[52,4,144]{2,1,0:T(4,128)(2,1)} %get-tuple-element.13.a1, f32[4,52]{1,0:T(4,128)} %get-tuple-element.14.a2, f32[4,52]{1,0:T(4,128)} %get-tuple-element.15.a3), custom_call_target="tpu_custom_call" | custom-call | tf_op jit(solution)/shard_map/hand_on/pallas_call | solution.py:555

commit v4 on v3

--- a/solution.py
+++ b/solution.py
@@ -17,6 +17,7 @@
 V = 272
 D = 4608
 SH = 144
+PART = 80
 NEAR = (1, 7, 2, 6, 3, 5, 4)
 FAR = (4, 3, 5, 2, 6, 1, 7)
 
@@ -59,11 +60,11 @@
     weight_grad_ref, hidden_grad_ref, logprob_ref, scale_ref,
     hid, tgt, grd, pln, tgt_wide, grd_wide, spread, pad, h, w, wt, wt_in, wg, term, term_in, hot, hot_in,
     own, xtx, xrx, ztx, zrx, own_t, xtx_t, xrx_t, ztx_t, zrx_t,
-    ytx, yrx, rtx, rrx, atx, arx, tot_tx, tot_rx,
+    ytx, yrx, atx, arx, tot_tx, tot_rx,
     in_sem, o_sem,
-    gy_s, gy_r, gz_s, gz_r, gx_s, gx_r, gc_s, gc_r,
+    gy_s, gy_r, gz_s, gz_r, gx_s, gx_r, gxz_s, gc_s, gc_r,
     t_s, t_r, w_s, w_r, m_s, m_r, x_s, x_r, z_s, z_r, xt_s, xt_r, zt_s, zt_r,
-    y_s, y_r, r_s, r_r, a_s, a_r, b_s, b_r,
+    y_s, y_r, a_s, a_r,
 ):
     x, y, z, c = coords()
     q, x_hi, p, zq = lax.rem(x, 2), lax.div(x, 2), lax.rem(z, 2), lax.div(z, 2)
@@ -76,6 +77,8 @@
     peers = [dev(x, y + d, z, c) for d in range(1, 8)]
     peers += [dev(x + a, y, z, c + b) for a in range(4) for b in range(2) if a or b]
     peers += [dev(x + 2 * a, y, z + d, c) for d in range(1, 8) for a in range(2)]
+    peers += [dev(x + d, y, z + d, c) for d in (1, -1)]
+    peers += [dev(x + 2, y + d, z, c) for d in range(1, 8)]
     loads = [
         pltpu.make_async_copy(src, dst, in_sem.at[i])
         for i, (src, dst) in enumerate(
@@ -115,6 +118,11 @@
         t = shard(x_lo, yy)
         return rcopy(h.at[half, t], h.at[half, t], gx_s.at[half, yy], gx_r.at[half, yy], dev(x + along(yy), y, z, c))
 
+    def xz_copy(x_lo, yy, half):
+        t = shard(x_lo, yy)
+        to = dev(x + along(yy), y, z + along(yy), c)
+        return rcopy(h.at[half, t], h.at[half, t], gxz_s.at[yy], gx_r.at[half, yy], to)
+
     def c_copy(x_lo, yy, cc, half):
         t = x_lo * 16 + yy * 2 + cc
         i = x_lo * 8 + yy
@@ -140,8 +148,13 @@
     def to_z_t(x_lo, yy):
         return rcopy(ztx_t.at[x_lo, yy], zrx_t.at[x_lo, yy], zt_s.at[x_lo, yy], zt_r.at[x_lo, yy], dev(x, y, z + along(yy), c))
 
-    def to_y(frm, to):
-        return rcopy(ytx.at[to], yrx.at[frm], y_s.at[to], y_r.at[frm], dev(x, to, z, c))
+    def to_y(frm, to, a):
+        rows = pl.ds(pl.multiple_of(64 * lax.rem(x_hi + a, 2), 16), PART)
+        return rcopy(ytx.at[to, rows], yrx.at[x_hi, frm], y_s.at[a, to], y_r.at[x_hi, frm], dev(x + 2 * a, to, z, c))
+
+    def from_y(frm, a):
+        other_hi = lax.rem(x_hi + a, 2)
+        return rcopy(ytx.at[0, pl.ds(0, PART)], yrx.at[other_hi, frm], y_s.at[a, frm], y_r.at[other_hi, frm], dev(x + 2 * a, frm, z, c))
 
     def at_y(d):
         return lax.rem(y + d, 8)
@@ -187,31 +200,26 @@
     hot[...] = hit.astype(F32).astype(BF16)
     hot_in[...] = ((s_id * 32 + t_id + 1 - 2 * c) * V + entry == slot_target).astype(F32).astype(BF16)
 
-    def target_mine(i, _):
-        own_t[i] = from_mine(i, hot).astype(BF16)
-        return 0
-
     def target_rows(i, _):
+        i = lax.rem(other * 8 + i, 16)
         x_lo, yy = lax.div(i, 8), lax.rem(i, 8)
         w_copy(i).wait_recv()
-        keep, pass_on = halves(own_t[i].astype(F32) + from_theirs(i, hot_in))
-        own_t[i, :, 0:128] = keep.astype(BF16)
+        keep, pass_on = halves(from_mine(i, hot) + from_theirs(i, hot_in))
+        own_t[i] = keep.astype(BF16)
         ztx_t[x_lo, yy] = pass_on.astype(BF16)
         to_z_t(x_lo, yy).start()
         return 0
 
-    for n, d in enumerate(NEAR):
+    for d in NEAR:
         yy = at_y(d)
         y_copy(yy, y).wait_recv()
+        x_copy(q, yy, p).start()
+        xz_copy(q, yy, p).start()
         z_copy(yy, p).start()
-        x_copy(q, yy, p).start()
         c_copy(q, yy, c, p).start()
-        if n < 4:
-            lax.fori_loop(4 * n, 4 * n + 4, target_mine, 0)
     for n, d in enumerate(NEAR):
         yy = at_y(d)
         z_copy(yy, 1 - p).wait_recv()
-        x_copy(q, yy, 1 - p).start()
         c_copy(q, yy, c, 1 - p).start()
         x_copy(other, yy, p).wait_recv()
         c_copy(other, yy, c, p).start()
@@ -223,6 +231,15 @@
         x_copy(other, yy, 1 - p).wait_recv()
         c_copy(other, yy, c, 1 - p).start()
     lax.fori_loop(14, 16, target_rows, 0)
+
+    def send_x_t(yy, _):
+        to_z_t(other, yy).wait_recv()
+        i = other * 8 + yy
+        xtx_t[yy] = own_t[i] + zrx_t[other, yy]
+        to_x_t(yy).start()
+        return 0
+
+    lax.fori_loop(0, 8, send_x_t, 0)
 
     def columns(b):
         return jnp.concatenate(
@@ -311,15 +328,6 @@
         return 0
 
     lax.fori_loop(0, 4, keep_first, 0)
-
-    def send_x_t(yy, _):
-        to_z_t(other, yy).wait_recv()
-        i = other * 8 + yy
-        xtx_t[yy] = (own_t[i, :, 0:128].astype(F32) + zrx_t[other, yy].astype(F32)).astype(BF16)
-        to_x_t(yy).start()
-        return 0
-
-    lax.fori_loop(0, 8, send_x_t, 0)
 
     def send_second(k, _):
         ya, yb = part_a(k), part_b(k)
@@ -358,7 +366,7 @@
         i = q * 8 + yy
         to_z_t(q, yy).wait_recv()
         to_x_t(yy).wait_recv()
-        own_t[i, :, 0:128] = (own_t[i, :, 0:128].astype(F32) + zrx_t[q, yy].astype(F32) + xrx_t[yy].astype(F32)).astype(BF16)
+        own_t[i] = own_t[i] + zrx_t[q, yy] + xrx_t[yy]
         return 0
 
     lax.fori_loop(0, 8, ready_t, 0)
@@ -374,16 +382,21 @@
 
     def merged(yy):
         i = q * 8 + yy
-        return half_t * own_t[i, :, 0:128].astype(F32) - half_s * own[i, :, 0:128]
+        return half_t * own_t[i].astype(F32) - half_s * own[i, :, 0:128]
 
     def send_y(k, _):
         yy = lax.rem(y + k, 8)
         ytx[yy] = merged(yy).astype(BF16)
-        to_y(y, yy).start()
+        to_y(y, yy, 0).start()
+        to_y(y, yy, 1).start()
         return 0
 
     lax.fori_loop(1, 8, send_y, 0)
-    acc = merged(y)
+    mine = merged(y)
+    ytx[y] = mine.astype(BF16)
+    to_y(y, y, 1).start()
+    own[q * 8 + y, :, 0:128] = mine
+    acc = own[q * 8 + y, pl.ds(pl.multiple_of(64 * x_hi, 16), PART), 0:128]
 
     soft = (-(slot_grad * (exponent / total)) * curve).astype(BF16)
 
@@ -407,48 +420,22 @@
 
     for d in NEAR:
         yy = at_y(d)
-        to_y(yy, y).wait_recv()
-        acc = acc + yrx[yy].astype(F32)
-
-    def member(j):
-        return dev(2 * lax.rem(j, 2) + q, y, 2 * lax.div(j, 2) + p, c)
-
-    index = zq * 2 + x_hi
-    for j in range(8):
-        rtx[j, 0:16] = acc[16 * j : 16 * j + 16].astype(BF16)
-        rtx[j, 16:32] = acc[128:144].astype(BF16)
-
-    def to_member(frm, to):
-        return rcopy(rtx.at[to], rrx.at[frm], r_s.at[to], r_r.at[frm], member(to))
-
-    for d in FAR:
-        to_member(index, lax.rem(index + d, 8)).start()
-    rrx[index] = rtx[index]
-    for d in FAR:
-        to_member(lax.rem(index + d, 8), index).wait_recv()
-    done = rrx[0].astype(F32)
-    for j in range(1, 8):
-        done = done + rrx[j].astype(F32)
-    atx[...] = done.astype(BF16)
-
-    z2 = z + 1 - 2 * p
-    slot = pl.ds(pl.multiple_of(index * 16, 16), 16)
-    tail = pl.ds(128, 16)
-    arx[p, slot] = atx[0:16]
-    arx[p, tail] = atx[16:32]
-    tail_copy = rcopy(atx.at[pl.ds(16, 16)], arx.at[p, tail], b_s, b_r, dev(x, y, z2, c))
-    tail_copy.start()
+        for a in range(2):
+            from_y(yy, a).wait_recv()
+            acc = acc + yrx[lax.rem(x_hi + a, 2), yy].astype(F32)
+    from_y(y, 1).wait_recv()
+    acc = acc + yrx[1 - x_hi, y].astype(F32)
+
+    atx[...] = acc.astype(BF16)
+    arx[x_hi, z] = atx[...]
     mates = [(a, d) for d in FAR + (0,) for a in range(2) if a or d]
 
     def to_mate(n, a, d):
-        return rcopy(atx.at[pl.ds(0, 16)], arx.at[p, slot], a_s.at[n], a_r.at[n], dev(x + 2 * a, y, z + d, c))
+        return rcopy(atx, arx.at[x_hi, z], a_s.at[n], a_r.at[n], dev(x + 2 * a, y, z + d, c))
 
     def from_mate(n, a, d):
-        zz = lax.rem(z - d + 8, 8)
-        pp = lax.rem(zz, 2)
-        ii = lax.div(zz, 2) * 2 + lax.rem(x_hi + a, 2)
-        there = pl.ds(pl.multiple_of(ii * 16, 16), 16)
-        return rcopy(atx.at[pl.ds(0, 16)], arx.at[pp, there], a_s.at[n], a_r.at[n], dev(x + 2 * a, y, z - d, c))
+        there = arx.at[lax.rem(x_hi + a, 2), lax.rem(z - d + 8, 8)]
+        return rcopy(atx, there, a_s.at[n], a_r.at[n], dev(x + 2 * a, y, z - d, c))
 
     for n, (a, d) in enumerate(mates):
         to_mate(n, a, d).start()
@@ -457,11 +444,14 @@
         y_copy(y, at_y(d)).wait_send()
     for d in NEAR:
         z_copy(at_y(d), p).wait_send()
+        x_copy(q, at_y(d), p).wait_send()
+        xz_copy(q, at_y(d), p).wait_send()
     for d in (0,) + NEAR:
         for half in range(2):
-            x_copy(q, at_y(d), half).wait_send()
             for x_lo in range(2):
                 c_copy(x_lo, at_y(d), c, half).wait_send()
+    for half in range(2):
+        x_copy(q, y, half).wait_send()
     term_copy.wait_send()
 
     def drain(yy, _):
@@ -483,15 +473,21 @@
     lax.fori_loop(0, 8, drain, 0)
     lax.fori_loop(0, 4, drain_ab, 0)
     for d in FAR:
-        to_y(y, at_y(d)).wait_send()
-        to_member(index, lax.rem(index + d, 8)).wait_send()
+        for a in range(2):
+            to_y(y, at_y(d), a).wait_send()
+    to_y(y, y, 1).wait_send()
     wg_copy.wait()
     for n, (a, d) in enumerate(mates):
         from_mate(n, a, d).wait_recv()
         to_mate(n, a, d).wait_send()
-    rcopy(atx.at[pl.ds(16, 16)], arx.at[1 - p, tail], b_s, b_r, dev(x, y, z2, c)).wait()
     for half in range(2):
-        wide = jnp.concatenate([arx[half].astype(F32), jnp.zeros((256 - SH, 128), F32)], axis=0)
+        parts = []
+        for hi in range(2):
+            part = arx[hi, half].astype(F32)
+            for k in range(1, 4):
+                part = part + arx[hi, 2 * k + half].astype(F32)
+            parts.append(part)
+        wide = jnp.concatenate([parts[0], parts[1][2 * PART - SH :], jnp.zeros((256 - SH, 128), F32)], axis=0)
         flat = jnp.transpose(wide, (1, 0))
         for k in range(2):
             spread[:, half * 2 + k, :] = flat[k * SLOT : k * SLOT + ROWS, 0:SH]
@@ -540,14 +536,14 @@
             buf(2, 32, *piece), buf(V, D), buf(D, V), buf(16, SH, V), buf(V, D),
             buf(V, 256), buf(V, 256), buf(V, 256), buf(V, 256),
             buf(16, SH, 256, dtype=F32), buf(2, 8, *piece), buf(2, 8, *piece), buf(2, 8, *piece), buf(2, 8, *piece),
-            buf(16, SH, 256), buf(8, *piece), buf(8, *piece), buf(2, 8, *piece), buf(2, 8, *piece),
-            buf(8, *piece), buf(8, *piece), buf(8, 32, 128), buf(8, 32, 128), buf(32, 128), buf(2, *piece),
+            buf(16, *piece), buf(8, *piece), buf(8, *piece), buf(2, 8, *piece), buf(2, 8, *piece),
+            buf(8, *piece), buf(2, 8, PART, 128), buf(PART, 128), buf(2, 8, PART, 128),
             buf(3, 2, 256, dtype=F32), buf(3, 8, 2, 256, dtype=F32),
             dma((5,)), dma,
-            dma((8,)), dma((8,)), dma((8,)), dma((8,)), dma((2, 8)), dma((2, 8)), dma((2, 16)), dma((2, 16)),
+            dma((8,)), dma((8,)), dma((8,)), dma((8,)), dma((2, 8)), dma((2, 8)), dma((8,)), dma((2, 16)), dma((2, 16)),
             dma((3, 8)), dma((3, 8)), dma((16,)), dma((16,)), dma, dma,
             dma((2, 8)), dma((2, 8)), dma((2, 8)), dma((2, 8)), dma((8,)), dma((8,)), dma((2, 8)), dma((2, 8)),
-            dma((8,)), dma((8,)), dma((8,)), dma((8,)), dma((15,)), dma((15,)), dma, dma,
+            dma((2, 8)), dma((2, 8)), dma((15,)), dma((15,)),
         ],
         compiler_params=pltpu.CompilerParams(collective_id=0, has_side_effects=True, vmem_limit_bytes=62 << 20),
         name="gather_logits_reduce",

time: 75 us -> 74.3 us (level)
  the two profiles are of different devices: /device:TPU:48 before, /device:TPU:16 now
where the time goes in v4:
time: 74.3 us; the launch traced here: 74.1 us
  Pallas kernels  73.5 us (99%)
    pallas_call x1, Pallas kernels, per_device(): pl.pallas_call(comm_kernel, out_shape=outs, in_specs=[hbm] * 5, out_specs...  70.8 us
    pallas_call x1, Pallas kernels, per_device(): pl.pallas_call(hand_on_kernel, out_shape=outs, in_specs=[hbm] * 4, out_sp...  2.66 us

profile of v4, /device:TPU:16, one launch (start us, length us, event | category | flops | bytes accessed | tf_op | source)
XLA Modules:
  0.0 74.1 jit_solution(6868760955106914201)
XLA Ops:
  0.6 70.8 %gather_logits_reduce.1 = (bf16[272,4608]{1,0:T(8,128)(2,1)}, bf16[52,4,144]{2,1,0:T(4,128)(2,1)}, f32[4,52]{1,0:T(4,128)}, f32[4,52]{1,0:T(4,128)}) custom-call(bf16[52,4,144]{2,1,0:T(4,128)(2,1)} %bitcast.2, bf16[272,4608]{1,0:T(8,128)(2,1)} %weight_ref.1, s32[4,52]{1,0:T(4,128)} %targets_ref.1, s32[4]{0:T(128)} %plan_ref.1, f32[4,52]{1,0:T(4,128)} %grad_ref.1), custom_call_target="tpu_custom_call" | custom-call | tf_op jit(solution)/shard_map/gather_logits_reduce/pallas_call | solution.py:526
  71.4 2.7 %hand_on.1 = (bf16[272,4608]{1,0:T(8,128)(2,1)}, bf16[52,4,144]{2,1,0:T(4,128)(2,1)}, f32[4,52]{1,0:T(4,128)}, f32[4,52]{1,0:T(4,128)}) custom-call(bf16[272,4608]{1,0:T(8,128)(2,1)} %get-tuple-element.12.a0, bf16[52,4,144]{2,1,0:T(4,128)(2,1)} %get-tuple-element.13.a1, f32[4,52]{1,0:T(4,128)} %get-tuple-element.14.a2, f32[4,52]{1,0:T(4,128)} %get-tuple-element.15.a3), custom_call_target="tpu_custom_call" | custom-call | tf_op jit(solution)/shard_map/hand_on/pallas_call | solution.py:551

commit v5 on v4

--- a/solution.py
+++ b/solution.py
@@ -142,8 +142,8 @@
     def to_z(x_lo, yy):
         return rcopy(ztx.at[x_lo, yy], zrx.at[x_lo, yy], z_s.at[x_lo, yy], z_r.at[x_lo, yy], dev(x, y, z + along(yy), c))
 
-    def to_x_t(yy):
-        return rcopy(xtx_t.at[yy], xrx_t.at[yy], xt_s.at[yy], xt_r.at[yy], dev(x + along(yy), y, z, c))
+    def to_x_t(half, yy, way):
+        return rcopy(xtx_t.at[half, yy], xrx_t.at[half, yy], xt_s.at[half, yy], xt_r.at[half, yy], dev(x + way, y, z, c))
 
     def to_z_t(x_lo, yy):
         return rcopy(ztx_t.at[x_lo, yy], zrx_t.at[x_lo, yy], zt_s.at[x_lo, yy], zt_r.at[x_lo, yy], dev(x, y, z + along(yy), c))
@@ -200,14 +200,27 @@
     hot[...] = hit.astype(F32).astype(BF16)
     hot_in[...] = ((s_id * 32 + t_id + 1 - 2 * c) * V + entry == slot_target).astype(F32).astype(BF16)
 
-    def target_rows(i, _):
-        i = lax.rem(other * 8 + i, 16)
-        x_lo, yy = lax.div(i, 8), lax.rem(i, 8)
+    def target_rows(i):
         w_copy(i).wait_recv()
-        keep, pass_on = halves(from_mine(i, hot) + from_theirs(i, hot_in))
-        own_t[i] = keep.astype(BF16)
-        ztx_t[x_lo, yy] = pass_on.astype(BF16)
-        to_z_t(x_lo, yy).start()
+        return from_mine(i, hot) + from_theirs(i, hot_in)
+
+    def target_first(k, _):
+        ya, yb = part_a(k), part_b(k)
+        value = target_rows(other * 8 + ya).astype(BF16)
+        for half in range(2):
+            xtx_t[half, ya] = value[:, half * 128 : (half + 1) * 128]
+            to_x_t(half, ya, 1 - 2 * half).start()
+        for x_lo in (other, q):
+            i = x_lo * 8 + yb
+            keep, pass_on = halves(target_rows(i))
+            ztx_t[x_lo, yb] = pass_on.astype(BF16)
+            to_z_t(x_lo, yb).start()
+            own_t[i, :, 0:128] = keep.astype(BF16)
+        return 0
+
+    def target_keep(k, _):
+        i = q * 8 + part_a(k)
+        own_t[i] = target_rows(i).astype(BF16)
         return 0
 
     for d in NEAR:
@@ -223,23 +236,32 @@
         c_copy(q, yy, c, 1 - p).start()
         x_copy(other, yy, p).wait_recv()
         c_copy(other, yy, c, p).start()
-        lax.fori_loop(2 * n, 2 * n + 2, target_rows, 0)
+        if n < 4:
+            target_first(n, 0)
+        elif n < 6:
+            lax.fori_loop(2 * n - 8, 2 * n - 6, target_keep, 0)
     x_copy(other, y, p).wait_recv()
     c_copy(other, y, c, p).start()
     for d in (0,) + NEAR:
         yy = at_y(d)
         x_copy(other, yy, 1 - p).wait_recv()
         c_copy(other, yy, c, 1 - p).start()
-    lax.fori_loop(14, 16, target_rows, 0)
-
-    def send_x_t(yy, _):
-        to_z_t(other, yy).wait_recv()
-        i = other * 8 + yy
-        xtx_t[yy] = own_t[i] + zrx_t[other, yy]
-        to_x_t(yy).start()
-        return 0
-
-    lax.fori_loop(0, 8, send_x_t, 0)
+
+    def target_second(k, _):
+        ya, yb = part_a(k), part_b(k)
+        to_z_t(other, yb).wait_recv()
+        xtx_t[0, yb] = own_t[other * 8 + yb, :, 0:128] + zrx_t[other, yb]
+        to_x_t(0, yb, along(yb)).start()
+        i = q * 8 + ya
+        for half in range(2):
+            to_x_t(half, ya, 1 - 2 * half).wait_recv()
+        both = own_t[i] + jnp.concatenate([xrx_t[0, ya], xrx_t[1, ya]], axis=1)
+        keep, pass_on = halves(both.astype(F32))
+        ztx_t[0, ya] = pass_on.astype(BF16)
+        to_z_t(0, ya).start()
+        own_t[i, :, 0:128] = keep.astype(BF16)
+        return 0
+
 
     def columns(b):
         return jnp.concatenate(
@@ -302,6 +324,7 @@
         return 0
 
     lax.fori_loop(0, 4, mine_first, 0)
+    lax.fori_loop(0, 4, target_second, 0)
     term_copy.wait_recv()
 
     def send_first(k, _):
@@ -362,14 +385,17 @@
         own[i, :, 0:128] = own[i, :, 0:128] + zrx[q, yy].astype(F32) + xrx[0, yy].astype(F32)
         return 0
 
-    def ready_t(yy, _):
-        i = q * 8 + yy
+    def ready_t(k, _):
+        i, yy = q * 8 + part_a(k), part_a(k)
+        to_z_t(0, yy).wait_recv()
+        own_t[i, :, 0:128] = own_t[i, :, 0:128] + zrx_t[0, yy]
+        i, yy = q * 8 + part_b(k), part_b(k)
         to_z_t(q, yy).wait_recv()
-        to_x_t(yy).wait_recv()
-        own_t[i] = own_t[i] + zrx_t[q, yy] + xrx_t[yy]
-        return 0
-
-    lax.fori_loop(0, 8, ready_t, 0)
+        to_x_t(0, yy, along(yy)).wait_recv()
+        own_t[i, :, 0:128] = own_t[i, :, 0:128] + zrx_t[q, yy] + xrx_t[0, yy]
+        return 0
+
+    lax.fori_loop(0, 4, ready_t, 0)
     lax.fori_loop(0, 4, ready_a, 0)
     lax.fori_loop(0, 4, ready_b, 0)
     sums = end(2)
@@ -382,7 +408,7 @@
 
     def merged(yy):
         i = q * 8 + yy
-        return half_t * own_t[i].astype(F32) - half_s * own[i, :, 0:128]
+        return half_t * own_t[i, :, 0:128].astype(F32) - half_s * own[i, :, 0:128]
 
     def send_y(k, _):
         yy = lax.rem(y + k, 8)
@@ -455,10 +481,8 @@
     term_copy.wait_send()
 
     def drain(yy, _):
-        to_x_t(yy).wait_send()
         for x_lo in range(2):
             w_copy(x_lo * 8 + yy).wait_send()
-            to_z_t(x_lo, yy).wait_send()
         return 0
 
     def drain_ab(k, _):
@@ -466,8 +490,12 @@
         for half in range(2):
             to_x(half, ya, 1 - 2 * half).wait_send()
             to_z(half, yb).wait_send()
+            to_x_t(half, ya, 1 - 2 * half).wait_send()
+            to_z_t(half, yb).wait_send()
         to_z(0, ya).wait_send()
         to_x(0, yb, along(yb)).wait_send()
+        to_z_t(0, ya).wait_send()
+        to_x_t(0, yb, along(yb)).wait_send()
         return 0
 
     lax.fori_loop(0, 8, drain, 0)
@@ -536,13 +564,13 @@
             buf(2, 32, *piece), buf(V, D), buf(D, V), buf(16, SH, V), buf(V, D),
             buf(V, 256), buf(V, 256), buf(V, 256), buf(V, 256),
             buf(16, SH, 256, dtype=F32), buf(2, 8, *piece), buf(2, 8, *piece), buf(2, 8, *piece), buf(2, 8, *piece),
-            buf(16, *piece), buf(8, *piece), buf(8, *piece), buf(2, 8, *piece), buf(2, 8, *piece),
+            buf(16, SH, 256), buf(2, 8, *piece), buf(2, 8, *piece), buf(2, 8, *piece), buf(2, 8, *piece),
             buf(8, *piece), buf(2, 8, PART, 128), buf(PART, 128), buf(2, 8, PART, 128),
             buf(3, 2, 256, dtype=F32), buf(3, 8, 2, 256, dtype=F32),
             dma((5,)), dma,
             dma((8,)), dma((8,)), dma((8,)), dma((8,)), dma((2, 8)), dma((2, 8)), dma((8,)), dma((2, 16)), dma((2, 16)),
             dma((3, 8)), dma((3, 8)), dma((16,)), dma((16,)), dma, dma,
-            dma((2, 8)), dma((2, 8)), dma((2, 8)), dma((2, 8)), dma((8,)), dma((8,)), dma((2, 8)), dma((2, 8)),
+            dma((2, 8)), dma((2, 8)), dma((2, 8)), dma((2, 8)), dma((2, 8)), dma((2, 8)), dma((2, 8)), dma((2, 8)),
             dma((2, 8)), dma((2, 8)), dma((15,)), dma((15,)),
         ],
         compiler_params=pltpu.CompilerParams(collective_id=0, has_side_effects=True, vmem_limit_bytes=62 << 20),

time: 74.3 us -> 73.5 us (0.989)
  the two profiles are of different devices: /device:TPU:16 before, /device:TPU:2 now
where the time goes in v5:
time: 73.5 us; the launch traced here: 73.3 us
  Pallas kernels  72.6 us (99%)
    pallas_call x1, Pallas kernels, per_device(): pl.pallas_call(comm_kernel, out_shape=outs, in_specs=[hbm] * 5, out_specs...  70 us
    pallas_call x1, Pallas kernels, per_device(): pl.pallas_call(hand_on_kernel, out_shape=outs, in_specs=[hbm] * 4, out_sp...  2.66 us

profile of v5, /device:TPU:2, one launch (start us, length us, event | category | flops | bytes accessed | tf_op | source)
XLA Modules:
  0.0 73.3 jit_solution(5790121885822084170)
XLA Ops:
  0.6 70.0 %gather_logits_reduce.1 = (bf16[272,4608]{1,0:T(8,128)(2,1)}, bf16[52,4,144]{2,1,0:T(4,128)(2,1)}, f32[4,52]{1,0:T(4,128)}, f32[4,52]{1,0:T(4,128)}) custom-call(bf16[52,4,144]{2,1,0:T(4,128)(2,1)} %bitcast.2, bf16[272,4608]{1,0:T(8,128)(2,1)} %weight_ref.1, s32[4,52]{1,0:T(4,128)} %targets_ref.1, s32[4]{0:T(128)} %plan_ref.1, f32[4,52]{1,0:T(4,128)} %grad_ref.1), custom_call_target="tpu_custom_call" | custom-call | tf_op jit(solution)/shard_map/gather_logits_reduce/pallas_call | solution.py:554
  70.6 2.7 %hand_on.1 = (bf16[272,4608]{1,0:T(8,128)(2,1)}, bf16[52,4,144]{2,1,0:T(4,128)(2,1)}, f32[4,52]{1,0:T(4,128)}, f32[4,52]{1,0:T(4,128)}) custom-call(bf16[272,4608]{1,0:T(8,128)(2,1)} %get-tuple-element.12.a0, bf16[52,4,144]{2,1,0:T(4,128)(2,1)} %get-tuple-element.13.a1, f32[4,52]{1,0:T(4,128)} %get-tuple-element.14.a2, f32[4,52]{1,0:T(4,128)} %get-tuple-element.15.a3), custom_call_target="tpu_custom_call" | custom-call | tf_op jit(solution)/shard_map/hand_on/pallas_call | solution.py:579

commit v6 on v5

--- a/solution.py
+++ b/solution.py
@@ -368,9 +368,8 @@
         own[i, :, 0:128] = keep
         return 0
 
-    lax.fori_loop(0, 2, send_second, 0)
     begin(2, end(1))
-    lax.fori_loop(2, 4, send_second, 0)
+    lax.fori_loop(0, 4, send_second, 0)
 
     def ready_a(k, _):
         i, yy = q * 8 + part_a(k), part_a(k)

time: 73.5 us -> 74.2 us (level)
  the two profiles are of different devices: /device:TPU:2 before, /device:TPU:1 now
where the time goes in v6:
time: 74.2 us; the launch traced here: 74 us
  Pallas kernels  73.4 us (99%)
    pallas_call x1, Pallas kernels, per_device(): pl.pallas_call(comm_kernel, out_shape=outs, in_specs=[hbm] * 5, out_specs...  70.7 us
    pallas_call x1, Pallas kernels, per_device(): pl.pallas_call(hand_on_kernel, out_shape=outs, in_specs=[hbm] * 4, out_sp...  2.66 us

profile of v6, /device:TPU:1, one launch (start us, length us, event | category | flops | bytes accessed | tf_op | source)
XLA Modules:
  0.0 74.0 jit_solution(6989772674397413214)
XLA Ops:
  0.6 70.7 %gather_logits_reduce.1 = (bf16[272,4608]{1,0:T(8,128)(2,1)}, bf16[52,4,144]{2,1,0:T(4,128)(2,1)}, f32[4,52]{1,0:T(4,128)}, f32[4,52]{1,0:T(4,128)}) custom-call(bf16[52,4,144]{2,1,0:T(4,128)(2,1)} %bitcast.2, bf16[272,4608]{1,0:T(8,128)(2,1)} %weight_ref.1, s32[4,52]{1,0:T(4,128)} %targets_ref.1, s32[4]{0:T(128)} %plan_ref.1, f32[4,52]{1,0:T(4,128)} %grad_ref.1), custom_call_target="tpu_custom_call" | custom-call | tf_op jit(solution)/shard_map/gather_logits_reduce/pallas_call | solution.py:553
  71.3 2.7 %hand_on.1 = (bf16[272,4608]{1,0:T(8,128)(2,1)}, bf16[52,4,144]{2,1,0:T(4,128)(2,1)}, f32[4,52]{1,0:T(4,128)}, f32[4,52]{1,0:T(4,128)}) custom-call(bf16[272,4608]{1,0:T(8,128)(2,1)} %get-tuple-element.12.a0, bf16[52,4,144]{2,1,0:T(4,128)(2,1)} %get-tuple-element.13.a1, f32[4,52]{1,0:T(4,128)} %get-tuple-element.14.a2, f32[4,52]{1,0:T(4,128)} %get-tuple-element.15.a3), custom_call_target="tpu_custom_call" | custom-call | tf_op jit(solution)/shard_map/hand_on/pallas_call | solution.py:578
